TPU v7x, 512 devices: a whole 4x8x8 slice. The times are simulated.
512 devices in a mesh: src: 32 (over z, x), tile: 16 (over y, core).
Axes of the slice: x: 4, y: 8, z: 8, core: 2. Of those that a mesh axis runs over, the one named last changes fastest.
Arguments:
- spectra: bfloat16 [32, 2, 128, 128], P('tile'), may hold values from -0.06 to 0.06
- pupils: bfloat16 [16, 128, 2, 128, 128], P('tile', 'src'), may hold values from -6 to 6
- zone_of: int32 [32], replicated, may hold values from 0 to 15
- density: int32 [32], replicated, may hold values from 1 to 4
- assignment: int32 [32], replicated, may hold values from 0 to 31, each once
- weights: int32 [128], P('src'), may hold values from 1 to 16
Outputs:
- intensity: float32 [128, 32, 2048], P('src', 'tile')
Inputs may be any that keep to these rules, and one draw needn't show every extreme that they name: `assignment`: a permutation of the tiles.
All inputs are finite; a program needn't handle non-finite values.
Results may differ from a plain program's by a relative error of at most 0.0018.
Values may be sent and summed in bfloat16 or wider, within the bound.
No kernel may reach another device: no remote copies, remote signals or barrier semaphores. Data moves between devices by JAX's collectives and lax.ppermute only.
A program may use at most 64 MiB of HBM per device.

v0:
```python
import math

import jax
import jax.numpy as jnp
from jax import lax
from jax.sharding import PartitionSpec as P

NPIX = 2048
ROWS = 128


def tables(freq_count, pixels, row_count):
    freq = jnp.arange(freq_count, dtype=jnp.int32) - freq_count // 2
    cols = jnp.arange(pixels, dtype=jnp.int32)
    angle = jnp.mod(freq[:, None] * cols[None, :], pixels).astype(jnp.float32) * (
        2.0 * math.pi / pixels
    )
    col_cos = jnp.cos(angle)
    col_sin = jnp.sin(angle)
    col_mat = jnp.concatenate(
        [jnp.concatenate([col_cos, col_sin], 1), jnp.concatenate([-col_sin, col_cos], 1)], 0
    ).astype(jnp.bfloat16)
    rws = jnp.arange(row_count, dtype=jnp.int32)
    phase = jnp.mod(rws[:, None] * freq[None, :], pixels).astype(jnp.float32) * (
        2.0 * math.pi / pixels
    )
    row_mat = jnp.concatenate([jnp.cos(phase), jnp.sin(phase)], 1).astype(jnp.bfloat16)
    return (col_mat, row_mat)


def half_field(pupil, spectrum, keep, col_mat):
    pupil_re = pupil[0].astype(jnp.float32)
    pupil_im = pupil[1].astype(jnp.float32)
    mask_re = spectrum[0].astype(jnp.float32)
    mask_im = spectrum[1].astype(jnp.float32)
    prod_re = (pupil_re * mask_re - pupil_im * mask_im) * keep
    prod_im = (pupil_re * mask_im + pupil_im * mask_re) * keep
    stacked = jnp.concatenate([prod_re, prod_im], 1).astype(jnp.bfloat16)
    return jnp.dot(stacked, col_mat, preferred_element_type=jnp.float32).astype(jnp.bfloat16)


def second_section(half):
    pixels = half.shape[1] // 2
    half_re = half[:, :pixels]
    half_im = half[:, pixels:]
    return jnp.concatenate([half, jnp.concatenate([-half_im, half_re], 1)], 0)


def power_of(second, row_mat):
    pixels = second.shape[1] // 2
    field = jnp.dot(row_mat, second, preferred_element_type=jnp.float32)
    return field[:, :pixels] * field[:, :pixels] + field[:, pixels:] * field[:, pixels:]


def shards(spectra, pupils, zone_of, density, assignment, weights):
    tile_count = spectra.shape[0]
    source_count = pupils.shape[1]
    freq_count = spectra.shape[-1]
    weight_f = weights.astype(jnp.float32)
    total = lax.psum(jnp.sum(weight_f), "src")
    every_spectrum = lax.all_gather(spectra, "tile", axis=0, tiled=True)
    slots = lax.axis_index("tile") * tile_count + jnp.arange(tile_count, dtype=jnp.int32)
    tiles = assignment[slots]
    zones = zone_of[tiles]
    levels = density[tiles]
    own_spectra = every_spectrum[tiles]
    every_pupil = lax.all_gather(pupils, "tile", axis=0, tiled=True)
    chosen = every_pupil[zones]
    freq = jnp.arange(freq_count, dtype=jnp.int32) - freq_count // 2
    keeps = (jnp.abs(freq)[None, :] * 8 < levels[:, None] * freq_count).astype(jnp.float32)
    col_mat, row_mat = tables(freq_count, NPIX, ROWS)
    images = []
    for slot in range(tile_count):
        keep = keeps[slot][:, None]
        accum = jnp.zeros((ROWS, NPIX), jnp.float32)
        for source in range(source_count):
            half = half_field(chosen[slot, source], own_spectra[slot], keep, col_mat)
            accum = accum + weight_f[source] * power_of(second_section(half), row_mat)
        images.append(accum)
    partial_value = jnp.stack(images, 1)
    summed = lax.psum_scatter(partial_value, "src", scatter_dimension=0, tiled=True)
    return summed / total


def solution(mesh):
    return jax.shard_map(
        shards,
        mesh=mesh,
        in_specs=(
            P("tile", None, None, None),
            P("tile", "src", None, None, None),
            P(),
            P(),
            P(),
            P("src"),
        ),
        out_specs=P("src", "tile", None),
        check_vma=False,
    )
```

profile of v0, /device:TPU:1, one launch (start us, length us, event | category | flops | bytes accessed | tf_op | source)
XLA Modules:
  0.0 292.3 jit_solution(9195662971775918408)
XLA Ops:
  6.5 0.7 all-gather.5.cloned.1.call-update
  7.3 0.7 all-gather.3.cloned.1.call-update
  8.1 0.6 gather_fusion
  8.7 1.3 gather_fusion.1
  10.0 1.3 gather_fusion.4
  11.3 0.7 convert_element_type.186
  12.0 0.6 fusion.177
  13.0 4.9 %fusion.79 = (bf16[128,2048]{1,0:T(8,128)(2,1)S(1)}, bf16[128,2048]{1,0:T(8,128)(2,1)S(1)}, bf16[128,2048]{1,0:T(8,128)(2,1)S(1)}) fusion(s32[128]{0:T(128)S(1)} %iota_add_fusion), kind=kLoop, calls=%fused_computation.123 | loop fusion | flops 4718592 | bytes 1573376 | tf_op jit(solution)/shard_map/convert.39
  17.9 39.4 %all-gather.5.cloned.1.call-done = bf16[32,2,128,128]{3,2,1,0:T(8,128)(2,1)} async-done(((bf16[2,2,128,128]{3,2,1,0:T(8,128)(2,1)}), bf16[32,2,128,128]{3,2,1,0:T(8,128)(2,1)}) %all-gather.5.cloned.1.call-update) | async-done | bytes 2097168 | tf_op jit(solution)/shard_map/all_gather | solution.py:61
  57.3 2.2 gather_fusion.3
  59.5 43.4 %all-gather.3.cloned.1.call-done = bf16[16,4,2,128,128]{4,3,2,1,0:T(8,128)(2,1)} async-done(((bf16[1,4,2,128,128]{4,3,2,1,0:T(8,128)(2,1)}), bf16[16,4,2,128,128]{4,3,2,1,0:T(8,128)(2,1)}) %all-gather.3.cloned.1.call-update) | async-done | bytes 4194320 | tf_op jit(solution)/shard_map/all_gather | solution.py:67
  102.9 2.8 gather_fusion.2
  106.2 0.5 convolution_convert_fusion.7
  110.0 0.5 convolution_convert_fusion
  114.2 3.5 %fusion.66 = f32[128,1,2048]{2,0,1:T(8,128)S(1)} fusion(f32[128,4096]{1,0:T(8,128)S(1)} %fusion.18, f32[128,4096]{1,0:T(8,128)S(1)} %fusion.12, f32[128,4096]{1,0:T(8,128)S(1)} %fusion.6, f32[128,4096]{1,0:T(8,128)S(1)} %fusion, f32[]{:T(128)} %bitcast.25, f32[]{:T(128)} %bitcast.20, f32[]{:T(128)} %bitcast.15, f32[]{:T(128)} %bitcast), kind=kLoop, calls=%fused_computation.93 | loop fusion | flops 4980736 | bytes 9437200 | tf_op jit(solution)/shard_map/stack | solution.py:80
  117.7 3.5 %fusion.54 = f32[128,1,2048]{2,0,1:T(8,128)S(1)} fusion(f32[128,4096]{1,0:T(8,128)S(1)} %fusion.42, f32[128,4096]{1,0:T(8,128)S(1)} %fusion.36, f32[128,4096]{1,0:T(8,128)S(1)} %fusion.30, f32[128,4096]{1,0:T(8,128)S(1)} %fusion.24, f32[]{:T(128)} %bitcast.25, f32[]{:T(128)} %bitcast.20, f32[]{:T(128)} %bitcast.15, f32[]{:T(128)} %bitcast), kind=kLoop, calls=%fused_computation.73 | loop fusion | flops 4980736 | bytes 9437200 | tf_op jit(solution)/shard_map/stack | solution.py:80
  121.3 1.5 pad_maximum_fusion
  122.9 0.6 copy-done.1
  123.5 0.6 convert_reduce_fusion
  124.1 62.7 %psum.7 = f32[]{:T(128)} all-reduce(f32[]{:T(128)} %convert_reduce_fusion), channel_id=1, replica_groups=mesh['src'=32,'tile'=16] {'src'}, use_global_device_ids=true, to_apply=%region_2.3 | all-reduce | flops 1 | bytes 8 | tf_op jit(solution)/shard_map/psum | solution.py:60
  186.7 1.3 dynamic-slice
  188.7 94.8 %all-reduce.3.cloned.1.call-done = f32[128,2,2048]{2,0,1:T(8,128)} async-done(((f32[128,2,2048]{2,0,1:T(8,128)}), f32[128,2,2048]{2,0,1:T(8,128)}) %all-reduce.3.cloned.1.call-update) | async-done | bytes 2097168
  283.5 1.5 dynamic-slice_divide_fusion
  285.0 0.7 copy.9
  (45 shorter events, 7.8 us)
Async XLA Ops:
  6.5 1.6 copy-start
  6.5 50.8 %all-gather.5.cloned.1.call-start = ((), (), s32[]{:S(2)}) async-start(), calls=%async_computation.1 | async-start | bytes 2228224 | tf_op jit(solution)/shard_map/all_gather | solution.py:61
  7.3 95.7 %all-gather.3.cloned.1.call-start = ((), (), s32[]{:S(2)}) async-start(), calls=%async_computation | async-start | bytes 4456448 | tf_op jit(solution)/shard_map/all_gather | solution.py:67
  8.0 275.5 %all-reduce.3.cloned.1.call-start = ((), (), s32[]{:S(2)}) async-start(), calls=%async_computation.2 | async-start | bytes 4194304
  122.8 0.7 copy-start.1
Sparse Core Ops, SparseCore 0:
  9.5 47.7 all-gather.4
  59.4 43.4 all-gather.2
  123.0 160.4 all-reduce.2
where the time goes:
time: 296 us; the launch traced here: 292 us
  waiting for transfers between devices  179 us (60%)
  blocking collectives  62.7 us (21%)
  other arithmetic  17.7 us (6%)
  between operations  14 us (5%)
  local copies, waits for them, and re-layouts  11.4 us (4%)
  matrix products  7.29 us (2%)
    unnamed x4, waiting for transfers between devices  96.3 us
    psum x1, blocking collectives, shards(): total = lax.psum(jnp.sum(weight_f), 'src')  62.7 us
    all_gather x1, waiting for transfers between devices, shards(): every_pupil = lax.all_gather(pupils, 'tile', axis=0, tiled=True)  43.4 us
    all_gather x1, waiting for transfers between devices, shards(): every_spectrum = lax.all_gather(spectra, 'tile', axis=0, tiled=True)  39.4 us
    another operation x3, other arithmetic, shards(): partial_value = jnp.stack(images, 1)  8.62 us
  transfers between devices with their start and end apart: 3, of which 3 were waited for; matrix products, arithmetic and copies ran while one was open for 5% of the time, Pallas kernels for 0%

commit v1 on v0

v1 whole, which is shorter than its diff:
```python
import math

import jax
import jax.numpy as jnp
import ml_dtypes
import numpy as np
from jax import lax
from jax.experimental import pallas as pl
from jax.experimental.pallas import tpu as pltpu
from jax.sharding import PartitionSpec as P

K = 128
NPIX = 2048
ROWS = 128
SAMPLES = 255
WIDE = 256
VMEM_LIMIT = 48 * 1024 * 1024


def sample_table():
    freq = np.arange(K) - K // 2
    point = np.arange(SAMPLES)
    angle = np.mod(freq[:, None] * point[None, :], SAMPLES) * (2.0 * math.pi / SAMPLES)
    table = np.zeros((K, 2 * WIDE))
    table[:, :SAMPLES] = np.cos(angle)
    table[:, WIDE : WIDE + SAMPLES] = np.sin(angle)
    return table.astype(ml_dtypes.bfloat16)


def row_tables(blocks):
    freq = np.arange(K) - K // 2
    place = np.arange(ROWS)
    group, lane = place // 8, place % 8
    even = lane % 2 == 0
    first = np.where(even, 8 * group + lane // 2, 8 * group + 4 + lane // 2)
    second = np.where(even, 8 * group + 4 + lane // 2, 8 * group + lane // 2)
    out = []
    for order in (first, second):
        phase = np.mod(order[:, None] * freq[None, :], NPIX) * (2.0 * math.pi / NPIX)
        both = np.stack([np.cos(phase), np.sin(phase)], 1).reshape(ROWS, 2, blocks, K // blocks)
        out.append(both.transpose(0, 2, 1, 3).reshape(ROWS, 2 * K))
    return np.stack(out).astype(ml_dtypes.bfloat16)


def interpolation_table():
    theta = 2.0 * math.pi * (np.arange(NPIX)[None, :] / NPIX - np.arange(SAMPLES)[:, None] / SAMPLES)
    half = np.sin(theta / 2)
    safe = np.where(np.abs(half) < 1e-12, 1.0, half)
    kernel = np.where(np.abs(half) < 1e-12, 1.0, np.sin(SAMPLES * theta / 2) / (SAMPLES * safe))
    table = np.zeros((WIDE, NPIX))
    table[:SAMPLES] = kernel
    high = table.astype(ml_dtypes.bfloat16)
    low = (table - high.astype(np.float64)).astype(ml_dtypes.bfloat16)
    return high, low


def product_kernel(assignment, zone_of, density, index, held, out):
    slots = assignment.shape[0]
    per_device = slots // out.shape[0]
    sources = 4
    freq = lax.broadcasted_iota(jnp.int32, (8, K), 0) + index[0] * 8 - K // 2
    distance = jnp.abs(freq) * 8
    for slot in range(slots):
        tile = assignment[slot]
        zone = zone_of[tile]
        keep = (distance < density[tile] * K).astype(jnp.float32)
        pupil = held[zone, 0:64, :].astype(jnp.float32).reshape(sources, 2, 8, K)
        start = pl.multiple_of(64 + 16 * (tile % 2), 16)
        mask = held[tile // 2, pl.ds(start, 16), :].astype(jnp.float32).reshape(2, 8, K)
        real = (pupil[:, 0] * mask[0] - pupil[:, 1] * mask[1]) * keep
        imag = (pupil[:, 0] * mask[1] + pupil[:, 1] * mask[0]) * keep
        both = jnp.stack([real, imag], 1).reshape(64, K).astype(jnp.bfloat16)
        out[slot // per_device, 64 * (slot % per_device) : 64 * (slot % per_device) + 64, :] = both


def image_kernel(weights, products, columns, rows, out):
    sources = 4
    blocks = products.shape[0]
    table = columns[...]
    images = []
    for slot in range(2):
        total = jnp.zeros((ROWS, WIDE), jnp.float32)
        for source in range(sources):
            start = (slot * sources + source) * 16
            product = products[:, start : start + 16, :].reshape(blocks * 16, K)
            half = jnp.dot(product, table, preferred_element_type=jnp.float32)
            half = half.reshape(blocks, 2, 8, 2 * WIDE)
            real = half[:, 0, :, :WIDE] - half[:, 1, :, WIDE:]
            imag = half[:, 0, :, WIDE:] + half[:, 1, :, :WIDE]
            upper = jnp.concatenate([real, imag], -1)
            lower = jnp.concatenate([-imag, real], -1)
            second = jnp.stack([upper, lower], 1).reshape(2 * K, 2 * WIDE).astype(jnp.bfloat16)
            field = jnp.dot(rows[slot], second, preferred_element_type=jnp.float32)
            power = field[:, :WIDE] * field[:, :WIDE] + field[:, WIDE:] * field[:, WIDE:]
            total = total + weights[source].astype(jnp.float32) * power
        images.append(total)
    weight_sum = weights[0] + weights[1] + weights[2] + weights[3]
    last = lax.broadcasted_iota(jnp.int32, (ROWS, WIDE), 1) == SAMPLES
    even = lax.broadcasted_iota(jnp.int32, (ROWS, WIDE), 0) % 2 == 0
    first = jnp.where(last, weight_sum.astype(jnp.float32), images[0])
    second = jnp.where(last, weight_sum.astype(jnp.float32), images[1])
    lower = jnp.where(even, first, second).reshape(ROWS // 8, 8, WIDE)
    upper = jnp.where(even, pltpu.roll(first, ROWS - 1, 0), pltpu.roll(second, 1, 0)).reshape(ROWS // 8, 8, WIDE)
    out[...] = jnp.stack([lower, upper], 1).reshape(ROWS // 4, 8, WIDE)


def finish_kernel(parts, high, low, out):
    summed = jnp.sum(parts[...], 0)
    total = summed[:, SAMPLES:]
    coarse = summed.astype(jnp.bfloat16)
    fine = (summed - coarse.astype(jnp.float32)).astype(jnp.bfloat16)
    both = jnp.concatenate([coarse, fine], 0)
    by_high = jnp.dot(both, high[...], preferred_element_type=jnp.float32)
    by_low = jnp.dot(coarse, low[...], preferred_element_type=jnp.float32)
    result = (by_high[:8] + by_high[8:] + by_low) / total
    out[...] = result


def shards(spectra, pupils, zone_of, density, assignment, weights):
    devices = lax.axis_size("tile")
    sources = pupils.shape[1]
    scalars = pl.BlockSpec(memory_space=pltpu.SMEM)
    blocks = pl.BlockSpec(memory_space=pltpu.VMEM)
    params = pltpu.CompilerParams(vmem_limit_bytes=VMEM_LIMIT)

    pupil_rows = pupils[0].reshape(sources, 2, devices, 8, K).transpose(2, 0, 1, 3, 4).reshape(devices, sources * 16, K)
    mask_rows = spectra.reshape(2, 2, devices, 8, K).transpose(2, 0, 1, 3, 4).reshape(devices, 32, K)
    held = lax.all_to_all(jnp.concatenate([pupil_rows, mask_rows], 1), "tile", 0, 0, tiled=True)

    index = lax.axis_index("tile").astype(jnp.int32).reshape(1)
    products = pl.pallas_call(
        product_kernel,
        out_shape=jax.ShapeDtypeStruct((devices, 2 * sources * 16, K), jnp.bfloat16),
        in_specs=[scalars] * 4 + [blocks],
        out_specs=blocks,
        compiler_params=params,
        name="products",
    )(assignment, zone_of, density, index, held)
    products = lax.all_to_all(products, "tile", 0, 0, tiled=True)

    image = pl.pallas_call(
        image_kernel,
        out_shape=jax.ShapeDtypeStruct((ROWS // 4, 8, WIDE), jnp.float32),
        in_specs=[scalars] + [blocks] * 3,
        out_specs=blocks,
        compiler_params=params,
        name="images",
    )(weights, products, jnp.asarray(sample_table()), jnp.asarray(row_tables(devices)))
    parts = lax.all_to_all(image, "src", 0, 0, tiled=True)

    high, low = interpolation_table()
    result = pl.pallas_call(
        finish_kernel,
        out_shape=jax.ShapeDtypeStruct((8, NPIX), jnp.float32),
        in_specs=[blocks] * 3,
        out_specs=blocks,
        compiler_params=params,
        name="finish",
    )(parts, jnp.asarray(high), jnp.asarray(low))
    return result.reshape(4, 2, NPIX)


def solution(mesh):
    return jax.shard_map(
        shards,
        mesh=mesh,
        in_specs=(
            P("tile", None, None, None),
            P("tile", "src", None, None, None),
            P(),
            P(),
            P(),
            P("src"),
        ),
        out_specs=P("src", "tile", None),
        check_vma=False,
    )
```

time: 296 us -> 75.4 us (0.25); the launches traced: 292 us -> 75.1 us
  waiting for transfers between devices: 179 us -> 14.5 us
  blocking collectives: 62.7 us -> 43.9 us
  other arithmetic: 17.7 us -> 0.78 us
  between operations: 14 us -> 0.1 us
  starting transfers between devices: 0.08 us -> 10.2 us
  local copies, waits for them, and re-layouts: 11.4 us -> 1.8 us
  matrix products: 7.29 us -> 0 us
  Pallas kernels: 0 us -> 3.8 us
    unnamed x4 -> x0, waiting for transfers between devices: 96.3 us -> none
    all_gather x2 -> x0, waiting for transfers between devices: 82.9 us -> none  [the longest x1 43.4 us: shards(): every_pupil = lax.all_gather(pupils, 'tile', axis=0, tiled=True)]
    psum x1 -> x0, blocking collectives: 62.7 us -> none  [shards(): total = lax.psum(jnp.sum(weight_f), 'src')]
    all_to_all x0 -> x2, blocking collectives: none -> 43.9 us  [the longest x1 23.7 us: shards(): parts = lax.all_to_all(image, 'src', 0, 0, tiled=True)]
    all_to_all x0 -> x1, waiting for transfers between devices: none -> 14.5 us  [shards(): lax.all_to_all(jnp.concatenate([pupil_rows, mask_rows], 1), 'tile', 0, 0,...]
    another operation x9 -> x0, other arithmetic: 14.2 us -> none  [the longest x3 8.62 us: shards(): partial_value = jnp.stack(images, 1)]
    all_to_all x0 -> x1, starting transfers between devices: none -> 10.2 us  [shards(): lax.all_to_all(jnp.concatenate([pupil_rows, mask_rows], 1), 'tile', 0, 0,...]
    gather x5 -> x0, local copies, waits for them, and re-layouts: 8.22 us -> none  [the longest x1 2.83 us: shards(): chosen = every_pupil[zones]]
  transfers between devices with their start and end apart: 3 -> 1, of which waited for: 3 -> 1; matrix products, arithmetic and copies ran while one was open for 5% -> 0% of each run, Pallas kernels for 0% -> 0%
where the time goes in v1:
time: 75.4 us; the launch traced here: 75.1 us
  blocking collectives  43.9 us (58%)
  waiting for transfers between devices  14.5 us (19%)
  starting transfers between devices  10.2 us (14%)
  Pallas kernels  3.8 us (5%)
  local copies, waits for them, and re-layouts  1.8 us (2%)
  other arithmetic  0.78 us (1%)
    all_to_all x1, blocking collectives, shards(): parts = lax.all_to_all(image, 'src', 0, 0, tiled=True)  23.7 us
    all_to_all x1, blocking collectives, shards(): products = lax.all_to_all(products, 'tile', 0, 0, tiled=True)  20.2 us
    all_to_all x1, waiting for transfers between devices, shards(): lax.all_to_all(jnp.concatenate([pupil_rows, mask_rows], 1), 'tile', 0, 0,...  14.5 us
    all_to_all x1, starting transfers between devices, shards(): lax.all_to_all(jnp.concatenate([pupil_rows, mask_rows], 1), 'tile', 0, 0,...  10.2 us
    pallas_call x1, Pallas kernels, shards(): pl.pallas_call(image_kernel, out_shape=jax.ShapeDtypeStruct((ROWS // 4, 8...  2.57 us
  transfers between devices with their start and end apart: 1, of which 1 were waited for; matrix products, arithmetic and copies ran while one was open for 0% of the time, Pallas kernels for 0%

profile of v1, /device:TPU:1, one launch (start us, length us, event | category | flops | bytes accessed | tf_op | source)
XLA Modules:
  0.0 75.1 jit_solution(18209259704827791825)
XLA Ops:
  0.0 1.0 %copy.12 = bf16[2,2,16,8,128]{4,3,1,0,2:T(8,128)(2,1)S(1)} copy(bf16[2,2,16,8,128]{4,3,2,1,0:T(8,128)(2,1)} %bitcast.12) | data formatting | bytes 262144 | tf_op jit(solution)/shard_map/reshape | solution.py:127
  1.0 0.0 copy-done.8
  1.0 0.1 copy.11
  1.1 0.8 %pad_maximum_fusion = bf16[16,96,128]{2,1,0:T(8,128)(2,1)} fusion(bf16[16,32,128]{2,1,0:T(8,128)(2,1)S(1)} %bitcast.10, bf16[16,64,128]{2,1,0:T(8,128)(2,1)S(1)} %bitcast.9), kind=kLoop, calls=%fused_computation | loop fusion | flops 786432 | bytes 786432 | tf_op jit(solution)/shard_map/concatenate | solution.py:128
  1.9 10.2 %all-to-all-start = ((bf16[16,96,128]{2,1,0:T(8,128)(2,1)}), bf16[16,96,128]{2,1,0:T(8,128)(2,1)S(1)}, u32[]{:S(2)}, u32[]{:S(2)}) async-start(bf16[16,96,128]{2,1,0:T(8,128)(2,1)} %pad_maximum_fusion), calls=%async_computation | async-start | bytes 786432 | tf_op jit(solution)/shard_map/all_to_all | solution.py:128
  12.1 0.0 copy-start.5
  12.1 0.0 copy-start.6
  12.1 14.5 %all-to-all-done.held = bf16[16,96,128]{2,1,0:T(8,128)(2,1)S(1)} async-done(((bf16[16,96,128]{2,1,0:T(8,128)(2,1)}), bf16[16,96,128]{2,1,0:T(8,128)(2,1)S(1)}, u32[]{:S(2)}, u32[]{:S(2)}) %all-to-all-start) | async-done | bytes 393248 | tf_op jit(solution)/shard_map/all_to_all | solution.py:128
  26.6 0.0 copy-done.4
  26.6 0.0 copy-done.5
  26.6 0.0 copy-done.6
  26.6 0.0 copy-start.2
  26.6 0.0 copy-start.3
  26.7 0.0 copy-start.7
  26.7 0.8 %products.1 = bf16[16,128,128]{2,1,0:T(8,128)(2,1)S(1)} custom-call(s32[32]{0:T(128)S(1)} %copy-done.4, s32[32]{0:T(128)S(1)} %copy-done.5, s32[32]{0:T(128)S(1)} %copy-done.6, s32[1]{0:T(128)} %bitcast.index, bf16[16,96,128]{2,1,0:T(8,128)(2,1)S(1)} %all-to-all-done.held), custom_call_target="tpu_custom_call" | custom-call | tf_op jit(solution)/shard_map/products/pallas_call | solution.py:131
  27.5 0.0 copy-start.1
  27.5 20.2 %all_to_all.15.products = bf16[16,128,128]{2,1,0:T(8,128)(2,1)S(1)} all-to-all(bf16[16,128,128]{2,1,0:T(8,128)(2,1)S(1)} %products.1), channel_id=1, replica_groups=mesh['src'=32,'tile'=16] {'tile'}, dimensions={0} | all-to-all | bytes 1048576 | tf_op jit(solution)/shard_map/all_to_all | solution.py:139
  47.7 0.0 copy-done.3
  47.7 0.0 copy-start
  47.7 2.6 %images.1 = f32[32,8,256]{2,1,0:T(8,128)S(1)} custom-call(s32[4]{0:T(128)S(1)} %copy-done.7, bf16[16,128,128]{2,1,0:T(8,128)(2,1)S(1)} %all_to_all.15.products, bf16[128,512]{1,0:T(8,128)(2,1)S(1)} %copy-done.3, bf16[2,128,256]{2,1,0:T(8,128)(2,1)S(1)} %copy-done.2), custom_call_target="tpu_custom_call" | custom-call | tf_op jit(solution)/shard_map/images/pallas_call | solution.py:141
  50.3 23.7 %all_to_all.16.parts = f32[32,8,256]{2,1,0:T(8,128)S(1)} all-to-all(f32[32,8,256]{2,1,0:T(8,128)S(1)} %images.1), channel_id=1, replica_groups=mesh['src'=32,'tile'=16] {'src'}, dimensions={0} | all-to-all | bytes 524288 | tf_op jit(solution)/shard_map/all_to_all | solution.py:149
  74.0 0.0 copy-done.1
  74.0 0.4 finish.1
  74.4 0.7 reshape.19
  (5 shorter events, 0.0 us)
Async XLA Ops:
  0.0 1.0 %copy-start.8 = (bf16[1,4,2,128,128]{4,3,2,1,0:T(8,128)(2,1)S(1)}, bf16[1,4,2,128,128]{4,3,2,1,0:T(8,128)(2,1)}, u32[]{:S(2)}) copy-start(bf16[1,4,2,128,128]{4,3,2,1,0:T(8,128)(2,1)} %param.11) | copy-start | bytes 786436
  1.9 24.8 %all-to-all-start = ((bf16[16,96,128]{2,1,0:T(8,128)(2,1)}), bf16[16,96,128]{2,1,0:T(8,128)(2,1)S(1)}, u32[]{:S(2)}, u32[]{:S(2)}) async-start(bf16[16,96,128]{2,1,0:T(8,128)(2,1)} %pad_maximum_fusion), calls=%async_computation | async-start | bytes 786432 | tf_op jit(solution)/shard_map/all_to_all | solution.py:128
  12.1 14.6 %copy-start.4 = (s32[32]{0:T(128)S(1)}, s32[32]{0:T(128)}, u32[]{:S(2)}) copy-start(s32[32]{0:T(128)} %assignment.1) | copy-start | bytes 388
  12.1 14.5 %copy-start.5 = (s32[32]{0:T(128)S(1)}, s32[32]{0:T(128)}, u32[]{:S(2)}) copy-start(s32[32]{0:T(128)} %zone_of.1) | copy-start | bytes 388
  12.1 14.5 %copy-start.6 = (s32[32]{0:T(128)S(1)}, s32[32]{0:T(128)}, u32[]{:S(2)}) copy-start(s32[32]{0:T(128)} %density.1) | copy-start | bytes 388
  26.6 21.0 %copy-start.2 = (bf16[2,128,256]{2,1,0:T(8,128)(2,1)S(1)}, bf16[2,128,256]{2,1,0:T(8,128)(2,1)}, u32[]{:S(2)}) copy-start(bf16[2,128,256]{2,1,0:T(8,128)(2,1)} %constant.13.clone.rows) | copy-start | bytes 393220
  26.6 21.0 %copy-start.3 = (bf16[128,512]{1,0:T(8,128)(2,1)S(1)}, bf16[128,512]{1,0:T(8,128)(2,1)}, u32[]{:S(2)}) copy-start(bf16[128,512]{1,0:T(8,128)(2,1)} %constant.12.clone.columns) | copy-start | bytes 393220
  26.7 21.0 %copy-start.7 = (s32[4]{0:T(128)S(1)}, s32[4]{0:T(128)}, u32[]{:S(2)}) copy-start(s32[4]{0:T(128)} %weights.1) | copy-start | bytes 52
  27.5 46.5 %copy-start.1 = (bf16[256,2048]{1,0:T(8,128)(2,1)S(1)}, bf16[256,2048]{1,0:T(8,128)(2,1)}, u32[]{:S(2)}) copy-start(bf16[256,2048]{1,0:T(8,128)(2,1)} %constant.14.clone.high) | copy-start | bytes 3145732
  47.7 26.3 %copy-start = (bf16[256,2048]{1,0:T(8,128)(2,1)S(1)}, bf16[256,2048]{1,0:T(8,128)(2,1)}, u32[]{:S(2)}) copy-start(bf16[256,2048]{1,0:T(8,128)(2,1)} %constant.15.clone.low) | copy-start | bytes 3145732

commit v2 on v1

v2 whole, which is shorter than its diff:
```python
import math

import jax
import jax.numpy as jnp
import ml_dtypes
import numpy as np
from jax import lax
from jax.experimental import pallas as pl
from jax.experimental.pallas import tpu as pltpu
from jax.sharding import PartitionSpec as P

K = 128
NPIX = 2048
ROWS = 128
SAMPLES = 255
WIDE = 256
VMEM_LIMIT = 48 * 1024 * 1024


def sample_table():
    freq = np.arange(K) - K // 2
    point = np.arange(SAMPLES)
    angle = np.mod(freq[:, None] * point[None, :], SAMPLES) * (2.0 * math.pi / SAMPLES)
    table = np.zeros((2, K, 2, WIDE))
    table[0, :, 0, :SAMPLES] = np.cos(angle)
    table[0, :, 1, :SAMPLES] = np.sin(angle)
    table[1, :, 0, :SAMPLES] = -np.sin(angle)
    table[1, :, 1, :SAMPLES] = np.cos(angle)
    return table.reshape(2 * K, 2 * WIDE).astype(ml_dtypes.bfloat16)


def row_tables():
    freq = np.arange(K) - K // 2
    place = np.arange(ROWS)
    group, lane = place // 8, place % 8
    even = lane % 2 == 0
    first = np.where(even, 8 * group + lane // 2, 8 * group + 4 + lane // 2)
    second = np.where(even, 8 * group + 4 + lane // 2, 8 * group + lane // 2)
    out = []
    for order in (first, second):
        phase = np.mod(order[:, None] * freq[None, :], NPIX) * (2.0 * math.pi / NPIX)
        out.append(np.concatenate([np.cos(phase), np.sin(phase)], 1))
    return np.stack(out).astype(ml_dtypes.bfloat16)


def interpolation_table():
    theta = 2.0 * math.pi * (np.arange(NPIX)[None, :] / NPIX - np.arange(SAMPLES)[:, None] / SAMPLES)
    half = np.sin(theta / 2)
    safe = np.where(np.abs(half) < 1e-12, 1.0, half)
    kernel = np.where(np.abs(half) < 1e-12, 1.0, np.sin(SAMPLES * theta / 2) / (SAMPLES * safe))
    table = np.zeros((WIDE, NPIX))
    table[:SAMPLES] = kernel
    high = table.astype(ml_dtypes.bfloat16)
    low = (table - high.astype(np.float64)).astype(ml_dtypes.bfloat16)
    return high, low


def layout_kernel(pupils, spectra, out, done):
    copies = []
    for piece in range(12):
        source = pupils.at[piece // 2, piece % 2] if piece < 8 else spectra.at[(piece - 8) // 2, piece % 2]
        copies.append(pltpu.make_async_copy(source, out.at[:, piece], done.at[piece]))
    for copy in copies:
        copy.start()
    for copy in copies:
        copy.wait()


def product_kernel(assignment, zone_of, density, index, held, out):
    slots = assignment.shape[0]
    per_device = slots // out.shape[0]
    sources = 4
    freq = lax.broadcasted_iota(jnp.int32, (8, K), 0) + index[0] * 8 - K // 2
    distance = jnp.abs(freq) * 8
    for slot in range(slots):
        tile = assignment[slot]
        zone = zone_of[tile]
        keep = (distance < density[tile] * K).astype(jnp.float32)
        pupil = held[zone, 0:64, :].astype(jnp.float32).reshape(sources, 2, 8, K)
        start = pl.multiple_of(64 + 16 * (tile % 2), 16)
        mask = held[tile // 2, pl.ds(start, 16), :].astype(jnp.float32).reshape(2, 8, K) * keep
        real = pupil[:, 0] * mask[0] - pupil[:, 1] * mask[1]
        imag = pupil[:, 0] * mask[1] + pupil[:, 1] * mask[0]
        both = jnp.stack([real.reshape(2, 16, K), imag.reshape(2, 16, K)], 1).reshape(64, K)
        first = 64 * (slot % per_device)
        out[slot // per_device, first : first + 64, :] = both.astype(jnp.bfloat16)


def image_kernel(weights, products, columns, rows, out):
    table = columns[...]
    images = []
    for slot in range(2):
        total = jnp.zeros((ROWS, WIDE), jnp.float32)
        for pair in range(2):
            start = (slot * 2 + pair) * 32
            real = products[:, start : start + 16, :].reshape(2 * K, K)
            imag = products[:, start + 16 : start + 32, :].reshape(2 * K, K)
            halves = jnp.dot(jnp.concatenate([real, imag], 1), table, preferred_element_type=jnp.float32)
            halves = halves.reshape(K // 8, 2, 8, 2 * WIDE)
            for source in range(2):
                half = halves[:, source].reshape(K, 2 * WIDE)
                crossed = jnp.concatenate([-half[:, WIDE:], half[:, :WIDE]], 1)
                second = jnp.concatenate([half.astype(jnp.bfloat16), crossed.astype(jnp.bfloat16)], 0)
                field = jnp.dot(rows[slot], second, preferred_element_type=jnp.float32)
                power = field[:, :WIDE] * field[:, :WIDE] + field[:, WIDE:] * field[:, WIDE:]
                total = total + weights[pair * 2 + source].astype(jnp.float32) * power
        images.append(total)
    weight_sum = weights[0] + weights[1] + weights[2] + weights[3]
    last = lax.broadcasted_iota(jnp.int32, (ROWS, WIDE), 1) == SAMPLES
    even = lax.broadcasted_iota(jnp.int32, (ROWS, WIDE), 0) % 2 == 0
    first = jnp.where(last, weight_sum.astype(jnp.float32), images[0])
    second = jnp.where(last, weight_sum.astype(jnp.float32), images[1])
    lower = jnp.where(even, first, second).reshape(ROWS // 8, 8, WIDE)
    upper = jnp.where(even, pltpu.roll(first, ROWS - 1, 0), pltpu.roll(second, 1, 0)).reshape(ROWS // 8, 8, WIDE)
    out[...] = jnp.stack([lower, upper], 1).reshape(ROWS // 4, 8, WIDE).astype(out.dtype)


def finish_kernel(parts, high, low, out):
    summed = jnp.sum(parts[...].astype(jnp.float32), 0)
    total = summed[:, SAMPLES:]
    coarse = summed.astype(jnp.bfloat16)
    fine = (summed - coarse.astype(jnp.float32)).astype(jnp.bfloat16)
    both = jnp.concatenate([coarse, fine], 0)
    by_high = jnp.dot(both, high[...], preferred_element_type=jnp.float32)
    by_low = jnp.dot(coarse, low[...], preferred_element_type=jnp.float32)
    result = (by_high[:8] + by_high[8:] + by_low) / total
    for row in range(out.shape[0]):
        out[row] = result[2 * row : 2 * row + 2]


def shards(spectra, pupils, zone_of, density, assignment, weights):
    devices = lax.axis_size("tile")
    sources = pupils.shape[1]
    scalars = pl.BlockSpec(memory_space=pltpu.SMEM)
    blocks = pl.BlockSpec(memory_space=pltpu.VMEM)
    params = pltpu.CompilerParams(vmem_limit_bytes=VMEM_LIMIT)

    hbm = pl.BlockSpec(memory_space=pltpu.HBM)
    laid = pl.pallas_call(
        layout_kernel,
        out_shape=jax.ShapeDtypeStruct((devices, 12, 8, K), jnp.bfloat16),
        in_specs=[hbm, hbm],
        out_specs=blocks,
        scratch_shapes=[pltpu.SemaphoreType.DMA((12,))],
        compiler_params=params,
        name="layout",
    )(pupils.reshape(sources, 2, devices, 8, K), spectra.reshape(2, 2, devices, 8, K))
    held = lax.all_to_all(laid.reshape(devices, 96, K), "tile", 0, 0, tiled=True)

    index = lax.axis_index("tile").astype(jnp.int32).reshape(1)
    products = pl.pallas_call(
        product_kernel,
        out_shape=jax.ShapeDtypeStruct((devices, 2 * sources * 16, K), jnp.bfloat16),
        in_specs=[scalars] * 4 + [blocks],
        out_specs=blocks,
        compiler_params=params,
        name="products",
    )(assignment, zone_of, density, index, held)
    products = lax.all_to_all(products, "tile", 0, 0, tiled=True)

    image = pl.pallas_call(
        image_kernel,
        out_shape=jax.ShapeDtypeStruct((ROWS // 4, 8, WIDE), jnp.bfloat16),
        in_specs=[scalars] + [blocks] * 3,
        out_specs=blocks,
        compiler_params=params,
        name="images",
    )(weights, products, jnp.asarray(sample_table()), jnp.asarray(row_tables()))
    parts = lax.all_to_all(image, "src", 0, 0, tiled=True)

    high, low = interpolation_table()
    return pl.pallas_call(
        finish_kernel,
        out_shape=jax.ShapeDtypeStruct((4, 2, NPIX), jnp.float32),
        in_specs=[blocks] * 3,
        out_specs=blocks,
        compiler_params=params,
        name="finish",
    )(parts, jnp.asarray(high), jnp.asarray(low))


def solution(mesh):
    return jax.shard_map(
        shards,
        mesh=mesh,
        in_specs=(
            P("tile", None, None, None),
            P("tile", "src", None, None, None),
            P(),
            P(),
            P(),
            P("src"),
        ),
        out_specs=P("src", "tile", None),
        check_vma=False,
    )
```

time: 75.4 us -> 73.3 us (0.972)
  blocking collectives: 43.9 us -> 41.5 us
  Pallas kernels: 3.8 us -> 4.71 us
  other arithmetic: 0.78 us -> 0 us
    all_to_all x1, blocking collectives: 23.7 us -> 21.4 us  [shards(): parts = lax.all_to_all(image, 'src', 0, 0, tiled=True)]
    unnamed x18 -> x20, local copies, waits for them, and re-layouts: 0.09 us -> 1.9 us
    reshape x2 -> x0, local copies, waits for them, and re-layouts: 1.66 us -> none  [the longest x1 0.97 us: shards(): spectra.reshape(2, 2, devices, 8, K).transpose(2, 0, 1, 3, 4)]
    pallas_call x1 -> x2, Pallas kernels: 0.39 us -> 2 us  [the longest x1 1.05 us: shards(): pl.pallas_call(finish_kernel, out_shape=jax.ShapeDtypeStruct((4, 2, NPIX)...]
    concatenate x1 -> x0, other arithmetic: 0.78 us -> none  [shards(): jnp.concatenate([pupil_rows, mask_rows], 1)]
where the time goes in v2:
time: 73.3 us; the launch traced here: 73 us
  blocking collectives  41.5 us (57%)
  waiting for transfers between devices  14.5 us (20%)
  starting transfers between devices  10.2 us (14%)
  Pallas kernels  4.71 us (6%)
  local copies, waits for them, and re-layouts  1.9 us (3%)
    all_to_all x1, blocking collectives, shards(): parts = lax.all_to_all(image, 'src', 0, 0, tiled=True)  21.4 us
    all_to_all x1, blocking collectives, shards(): products = lax.all_to_all(products, 'tile', 0, 0, tiled=True)  20.2 us
    all_to_all x1, waiting for transfers between devices, shards(): lax.all_to_all(laid.reshape(devices, 96, K), 'tile', 0, 0, tiled=True)  14.5 us
    all_to_all x1, starting transfers between devices, shards(): lax.all_to_all(laid.reshape(devices, 96, K), 'tile', 0, 0, tiled=True)  10.2 us
    unnamed x20, local copies, waits for them, and re-layouts  1.9 us
    pallas_call x1, Pallas kernels, shards(): pl.pallas_call(image_kernel, out_shape=jax.ShapeDtypeStruct((ROWS // 4, 8...  1.88 us
  transfers between devices with their start and end apart: 1, of which 1 were waited for; matrix products, arithmetic and copies ran while one was open for 0% of the time, Pallas kernels for 0%

profile of v2, /device:TPU:1, one launch (start us, length us, event | category | flops | bytes accessed | tf_op | source)
XLA Modules:
  0.0 73.0 jit_solution(216270102312549903)
XLA Ops:
  0.0 0.9 %copy-done.2 = bf16[1,4,2,128,128]{4,3,2,1,0:T(8,128)(2,1)S(1)} copy-done((bf16[1,4,2,128,128]{4,3,2,1,0:T(8,128)(2,1)S(1)}, bf16[1,4,2,128,128]{4,3,2,1,0:T(8,128)(2,1)}, u32[]{:S(2)}) %copy-start.2) | copy-done | bytes 262168
  1.0 0.9 %copy-done.4 = bf16[2,2,128,128]{3,2,1,0:T(8,128)(2,1)S(1)} copy-done((bf16[2,2,128,128]{3,2,1,0:T(8,128)(2,1)S(1)}, bf16[2,2,128,128]{3,2,1,0:T(8,128)(2,1)}, u32[]{:S(2)}) %copy-start.4) | copy-done | bytes 131096
  1.9 0.9 %layout.1 = bf16[16,12,8,128]{3,2,1,0:T(8,128)(2,1)} custom-call(bf16[4,2,16,8,128]{4,3,2,1,0:T(8,128)(2,1)S(1)} %bitcast.4, bf16[2,2,16,8,128]{4,3,2,1,0:T(8,128)(2,1)S(1)} %bitcast.5), custom_call_target="tpu_custom_call" | custom-call | tf_op jit(solution)/shard_map/layout/pallas_call | solution.py:139
  2.8 10.2 %all-to-all-start = ((bf16[16,96,128]{2,1,0:T(8,128)(2,1)}), bf16[16,96,128]{2,1,0:T(8,128)(2,1)S(1)}, u32[]{:S(2)}, u32[]{:S(2)}) async-start(bf16[16,96,128]{2,1,0:T(8,128)(2,1)} %bitcast.3), calls=%async_computation | async-start | bytes 786432 | tf_op jit(solution)/shard_map/all_to_all | solution.py:148
  13.0 0.0 copy-start.7
  13.1 0.0 copy-start.8
  13.1 14.5 %all-to-all-done.held = bf16[16,96,128]{2,1,0:T(8,128)(2,1)S(1)} async-done(((bf16[16,96,128]{2,1,0:T(8,128)(2,1)}), bf16[16,96,128]{2,1,0:T(8,128)(2,1)S(1)}, u32[]{:S(2)}, u32[]{:S(2)}) %all-to-all-start) | async-done | bytes 393248 | tf_op jit(solution)/shard_map/all_to_all | solution.py:148
  27.6 0.0 copy-done.6
  27.6 0.0 copy-done.7
  27.6 0.0 copy-done.8
  27.6 0.0 copy-start.3
  27.6 0.0 copy-start.5
  27.6 0.0 copy-start.9
  27.6 0.8 %products.1 = bf16[16,128,128]{2,1,0:T(8,128)(2,1)S(1)} custom-call(s32[32]{0:T(128)S(1)} %copy-done.6, s32[32]{0:T(128)S(1)} %copy-done.7, s32[32]{0:T(128)S(1)} %copy-done.8, s32[1]{0:T(128)} %bitcast.index, bf16[16,96,128]{2,1,0:T(8,128)(2,1)S(1)} %all-to-all-done.held), custom_call_target="tpu_custom_call" | custom-call | tf_op jit(solution)/shard_map/products/pallas_call | solution.py:151
  28.5 0.0 copy-start
  28.5 0.0 copy-start.1
  28.5 20.2 %all_to_all.15.products = bf16[16,128,128]{2,1,0:T(8,128)(2,1)S(1)} all-to-all(bf16[16,128,128]{2,1,0:T(8,128)(2,1)S(1)} %products.1), channel_id=1, replica_groups=mesh['src'=32,'tile'=16] {'tile'}, dimensions={0} | all-to-all | bytes 1048576 | tf_op jit(solution)/shard_map/all_to_all | solution.py:159
  48.7 0.0 copy-done.3
  48.7 0.0 copy-done.5
  48.7 0.0 copy-done.9
  48.7 1.9 %images.1 = bf16[32,8,256]{2,1,0:T(8,128)(2,1)S(1)} custom-call(s32[4]{0:T(128)S(1)} %copy-done.9, bf16[16,128,128]{2,1,0:T(8,128)(2,1)S(1)} %all_to_all.15.products, bf16[256,512]{1,0:T(8,128)(2,1)S(1)} %copy-done.3, bf16[2,128,256]{2,1,0:T(8,128)(2,1)S(1)} %copy-done.5), custom_call_target="tpu_custom_call" | custom-call | tf_op jit(solution)/shard_map/images/pallas_call | solution.py:161
  50.6 21.4 %all_to_all.16.parts = bf16[32,8,256]{2,1,0:T(8,128)(2,1)S(1)} all-to-all(bf16[32,8,256]{2,1,0:T(8,128)(2,1)S(1)} %images.1), channel_id=1, replica_groups=mesh['src'=32,'tile'=16] {'src'}, dimensions={0} | all-to-all | bytes 262144 | tf_op jit(solution)/shard_map/all_to_all | solution.py:169
  71.9 0.0 copy-done
  71.9 1.1 %finish.1 = f32[4,2,2048]{2,1,0:T(2,128)} custom-call(bf16[32,8,256]{2,1,0:T(8,128)(2,1)S(1)} %all_to_all.16.parts, bf16[256,2048]{1,0:T(8,128)(2,1)S(1)} %copy-done.1, bf16[256,2048]{1,0:T(8,128)(2,1)S(1)} %copy-done), custom_call_target="tpu_custom_call" | custom-call | tf_op jit(solution)/shard_map/finish/pallas_call | solution.py:172
  (4 shorter events, 0.0 us)
Async XLA Ops:
  0.0 0.9 %copy-start.2 = (bf16[1,4,2,128,128]{4,3,2,1,0:T(8,128)(2,1)S(1)}, bf16[1,4,2,128,128]{4,3,2,1,0:T(8,128)(2,1)}, u32[]{:S(2)}) copy-start(bf16[1,4,2,128,128]{4,3,2,1,0:T(8,128)(2,1)} %param.11) | copy-start | bytes 786436
  1.0 0.9 %copy-start.4 = (bf16[2,2,128,128]{3,2,1,0:T(8,128)(2,1)S(1)}, bf16[2,2,128,128]{3,2,1,0:T(8,128)(2,1)}, u32[]{:S(2)}) copy-start(bf16[2,2,128,128]{3,2,1,0:T(8,128)(2,1)} %param.10) | copy-start | bytes 393220
  2.8 24.8 %all-to-all-start = ((bf16[16,96,128]{2,1,0:T(8,128)(2,1)}), bf16[16,96,128]{2,1,0:T(8,128)(2,1)S(1)}, u32[]{:S(2)}, u32[]{:S(2)}) async-start(bf16[16,96,128]{2,1,0:T(8,128)(2,1)} %bitcast.3), calls=%async_computation | async-start | bytes 786432 | tf_op jit(solution)/shard_map/all_to_all | solution.py:148
  13.0 14.6 %copy-start.6 = (s32[32]{0:T(128)S(1)}, s32[32]{0:T(128)}, u32[]{:S(2)}) copy-start(s32[32]{0:T(128)} %assignment.1) | copy-start | bytes 388
  13.0 14.5 %copy-start.7 = (s32[32]{0:T(128)S(1)}, s32[32]{0:T(128)}, u32[]{:S(2)}) copy-start(s32[32]{0:T(128)} %zone_of.1) | copy-start | bytes 388
  13.1 14.5 %copy-start.8 = (s32[32]{0:T(128)S(1)}, s32[32]{0:T(128)}, u32[]{:S(2)}) copy-start(s32[32]{0:T(128)} %density.1) | copy-start | bytes 388
  27.6 21.1 %copy-start.3 = (bf16[256,512]{1,0:T(8,128)(2,1)S(1)}, bf16[256,512]{1,0:T(8,128)(2,1)}, u32[]{:S(2)}) copy-start(bf16[256,512]{1,0:T(8,128)(2,1)} %constant.12.clone.columns) | copy-start | bytes 786436
  27.6 21.0 %copy-start.5 = (bf16[2,128,256]{2,1,0:T(8,128)(2,1)S(1)}, bf16[2,128,256]{2,1,0:T(8,128)(2,1)}, u32[]{:S(2)}) copy-start(bf16[2,128,256]{2,1,0:T(8,128)(2,1)} %constant.13.clone.rows) | copy-start | bytes 393220
  27.6 21.0 %copy-start.9 = (s32[4]{0:T(128)S(1)}, s32[4]{0:T(128)}, u32[]{:S(2)}) copy-start(s32[4]{0:T(128)} %weights.1) | copy-start | bytes 52
  28.5 43.5 %copy-start = (bf16[256,2048]{1,0:T(8,128)(2,1)S(1)}, bf16[256,2048]{1,0:T(8,128)(2,1)}, u32[]{:S(2)}) copy-start(bf16[256,2048]{1,0:T(8,128)(2,1)} %constant.15.clone.low) | copy-start | bytes 3145732
  28.5 43.5 %copy-start.1 = (bf16[256,2048]{1,0:T(8,128)(2,1)S(1)}, bf16[256,2048]{1,0:T(8,128)(2,1)}, u32[]{:S(2)}) copy-start(bf16[256,2048]{1,0:T(8,128)(2,1)} %constant.14.clone.high) | copy-start | bytes 3145732

commit v3 on v2

--- a/solution.py
+++ b/solution.py
@@ -39,7 +39,8 @@
     out = []
     for order in (first, second):
         phase = np.mod(order[:, None] * freq[None, :], NPIX) * (2.0 * math.pi / NPIX)
-        out.append(np.concatenate([np.cos(phase), np.sin(phase)], 1))
+        cos, sin = np.cos(phase), np.sin(phase)
+        out.append(np.block([[cos, -sin], [sin, cos]]))
     return np.stack(out).astype(ml_dtypes.bfloat16)
 
 
@@ -66,11 +67,11 @@
         copy.wait()
 
 
-def product_kernel(assignment, zone_of, density, index, held, out):
+def product_kernel(assignment, zone_of, density, held, out):
     slots = assignment.shape[0]
     per_device = slots // out.shape[0]
     sources = 4
-    freq = lax.broadcasted_iota(jnp.int32, (8, K), 0) + index[0] * 8 - K // 2
+    freq = lax.broadcasted_iota(jnp.int32, (8, K), 0) + lax.axis_index("tile") * 8 - K // 2
     distance = jnp.abs(freq) * 8
     for slot in range(slots):
         tile = assignment[slot]
@@ -87,23 +88,24 @@
 
 
 def image_kernel(weights, products, columns, rows, out):
-    table = columns[...]
+    stacked = []
+    for piece in range(4):
+        real = products[:, 32 * piece : 32 * piece + 16, :].reshape(2 * K, K)
+        imag = products[:, 32 * piece + 16 : 32 * piece + 32, :].reshape(2 * K, K)
+        stacked.append(jnp.concatenate([real, imag], 1))
+    halves = jnp.dot(jnp.concatenate(stacked, 0), columns[...], preferred_element_type=jnp.float32)
+    halves = halves.reshape(2, 2, K // 8, 2, 8, 2 * WIDE)
     images = []
     for slot in range(2):
+        sides = []
+        for source in range(4):
+            half = halves[slot, source // 2, :, source % 2].reshape(K, 2 * WIDE).astype(jnp.bfloat16)
+            sides.append(jnp.concatenate([half[:, :WIDE], half[:, WIDE:]], 0))
+        field = jnp.dot(rows[slot], jnp.concatenate(sides, 1), preferred_element_type=jnp.float32)
+        power = field[:ROWS] * field[:ROWS] + field[ROWS:] * field[ROWS:]
         total = jnp.zeros((ROWS, WIDE), jnp.float32)
-        for pair in range(2):
-            start = (slot * 2 + pair) * 32
-            real = products[:, start : start + 16, :].reshape(2 * K, K)
-            imag = products[:, start + 16 : start + 32, :].reshape(2 * K, K)
-            halves = jnp.dot(jnp.concatenate([real, imag], 1), table, preferred_element_type=jnp.float32)
-            halves = halves.reshape(K // 8, 2, 8, 2 * WIDE)
-            for source in range(2):
-                half = halves[:, source].reshape(K, 2 * WIDE)
-                crossed = jnp.concatenate([-half[:, WIDE:], half[:, :WIDE]], 1)
-                second = jnp.concatenate([half.astype(jnp.bfloat16), crossed.astype(jnp.bfloat16)], 0)
-                field = jnp.dot(rows[slot], second, preferred_element_type=jnp.float32)
-                power = field[:, :WIDE] * field[:, :WIDE] + field[:, WIDE:] * field[:, WIDE:]
-                total = total + weights[pair * 2 + source].astype(jnp.float32) * power
+        for source in range(4):
+            total = total + weights[source].astype(jnp.float32) * power[:, source * WIDE : (source + 1) * WIDE]
         images.append(total)
     weight_sum = weights[0] + weights[1] + weights[2] + weights[3]
     last = lax.broadcasted_iota(jnp.int32, (ROWS, WIDE), 1) == SAMPLES
@@ -115,17 +117,26 @@
     out[...] = jnp.stack([lower, upper], 1).reshape(ROWS // 4, 8, WIDE).astype(out.dtype)
 
 
-def finish_kernel(parts, high, low, out):
+def finish_kernel(parts, high, low, out, held, done):
     summed = jnp.sum(parts[...].astype(jnp.float32), 0)
     total = summed[:, SAMPLES:]
     coarse = summed.astype(jnp.bfloat16)
     fine = (summed - coarse.astype(jnp.float32)).astype(jnp.bfloat16)
     both = jnp.concatenate([coarse, fine], 0)
-    by_high = jnp.dot(both, high[...], preferred_element_type=jnp.float32)
-    by_low = jnp.dot(coarse, low[...], preferred_element_type=jnp.float32)
-    result = (by_high[:8] + by_high[8:] + by_low) / total
-    for row in range(out.shape[0]):
-        out[row] = result[2 * row : 2 * row + 2]
+    copies = []
+    width = NPIX // 4
+    for piece in range(4):
+        cut = pl.ds(width * piece, width)
+        by_high = jnp.dot(both, high[:, cut], preferred_element_type=jnp.float32)
+        by_low = jnp.dot(coarse, low[:, cut], preferred_element_type=jnp.float32)
+        result = (by_high[:8] + by_high[8:] + by_low) / total
+        for row in range(4):
+            held[row, :, cut] = result[2 * row : 2 * row + 2]
+        copy = pltpu.make_async_copy(held.at[:, :, cut], out.at[:, :, cut], done.at[piece])
+        copy.start()
+        copies.append(copy)
+    for copy in copies:
+        copy.wait()
 
 
 def shards(spectra, pupils, zone_of, density, assignment, weights):
@@ -142,20 +153,18 @@
         in_specs=[hbm, hbm],
         out_specs=blocks,
         scratch_shapes=[pltpu.SemaphoreType.DMA((12,))],
-        compiler_params=params,
         name="layout",
     )(pupils.reshape(sources, 2, devices, 8, K), spectra.reshape(2, 2, devices, 8, K))
     held = lax.all_to_all(laid.reshape(devices, 96, K), "tile", 0, 0, tiled=True)
 
-    index = lax.axis_index("tile").astype(jnp.int32).reshape(1)
     products = pl.pallas_call(
         product_kernel,
         out_shape=jax.ShapeDtypeStruct((devices, 2 * sources * 16, K), jnp.bfloat16),
-        in_specs=[scalars] * 4 + [blocks],
+        in_specs=[scalars] * 3 + [blocks],
         out_specs=blocks,
         compiler_params=params,
         name="products",
-    )(assignment, zone_of, density, index, held)
+    )(assignment, zone_of, density, held)
     products = lax.all_to_all(products, "tile", 0, 0, tiled=True)
 
     image = pl.pallas_call(
@@ -173,7 +182,8 @@
         finish_kernel,
         out_shape=jax.ShapeDtypeStruct((4, 2, NPIX), jnp.float32),
         in_specs=[blocks] * 3,
-        out_specs=blocks,
+        out_specs=hbm,
+        scratch_shapes=[pltpu.VMEM((4, 2, NPIX), jnp.float32), pltpu.SemaphoreType.DMA((4,))],
         compiler_params=params,
         name="finish",
     )(parts, jnp.asarray(high), jnp.asarray(low))

time: 73.3 us -> 71.9 us (0.981)
  blocking collectives: 41.5 us -> 66.4 us
  waiting for transfers between devices: 14.5 us -> 0 us
  starting transfers between devices: 10.2 us -> 0 us
  local copies, waits for them, and re-layouts: 1.9 us -> 0.05 us
    all_to_all x0 -> x1, blocking collectives: none -> 24.9 us  [shards(): lax.all_to_all(laid.reshape(devices, 96, K), 'tile', 0, 0, tiled=True)]
    all_to_all x1 -> x0, waiting for transfers between devices: 14.5 us -> none  [shards(): lax.all_to_all(laid.reshape(devices, 96, K), 'tile', 0, 0, tiled=True)]
    all_to_all x1 -> x0, starting transfers between devices: 10.2 us -> none  [shards(): lax.all_to_all(laid.reshape(devices, 96, K), 'tile', 0, 0, tiled=True)]
    unnamed x20 -> x16, local copies, waits for them, and re-layouts: 1.9 us -> 0.05 us
    pallas_call x1, Pallas kernels: 0.94 us -> 1.78 us  [shards(): pl.pallas_call(layout_kernel, out_shape=jax.ShapeDtypeStruct((devices, 12...]
  transfers between devices with their start and end apart: 1 -> 0, of which waited for: 1 -> 0; matrix products, arithmetic and copies ran while one was open for 0% -> 0% of each run, Pallas kernels for 0% -> 0%
where the time goes in v3:
time: 71.9 us; the launch traced here: 71.5 us
  blocking collectives  66.4 us (92%)
  Pallas kernels  4.96 us (7%)
    all_to_all x1, blocking collectives, shards(): lax.all_to_all(laid.reshape(devices, 96, K), 'tile', 0, 0, tiled=True)  24.9 us
    all_to_all x1, blocking collectives, shards(): parts = lax.all_to_all(image, 'src', 0, 0, tiled=True)  21.4 us
    all_to_all x1, blocking collectives, shards(): products = lax.all_to_all(products, 'tile', 0, 0, tiled=True)  20.2 us
    pallas_call x1, Pallas kernels, shards(): pl.pallas_call(layout_kernel, out_shape=jax.ShapeDtypeStruct((devices, 12...  1.78 us

profile of v3, /device:TPU:1, one launch (start us, length us, event | category | flops | bytes accessed | tf_op | source)
XLA Modules:
  0.0 71.5 jit_solution(50985643813922768)
XLA Ops:
  0.0 1.8 %layout.1 = bf16[16,12,8,128]{3,2,1,0:T(8,128)(2,1)} custom-call(bf16[4,2,16,8,128]{4,3,2,1,0:T(8,128)(2,1)} %bitcast.4, bf16[2,2,16,8,128]{4,3,2,1,0:T(8,128)(2,1)} %bitcast.5), custom_call_target="tpu_custom_call" | custom-call | tf_op jit(solution)/shard_map/layout/pallas_call | solution.py:150
  1.8 0.0 copy-start.4
  1.8 0.0 copy-start.5
  1.8 0.0 copy-start.6
  1.8 24.9 %all_to_all.15.held = bf16[16,96,128]{2,1,0:T(8,128)(2,1)S(1)} all-to-all(bf16[16,96,128]{2,1,0:T(8,128)(2,1)} %bitcast.3), channel_id=1, replica_groups=mesh['src'=32,'tile'=16] {'tile'}, dimensions={0} | all-to-all | bytes 786432 | tf_op jit(solution)/shard_map/all_to_all | solution.py:158
  26.7 0.0 copy-done.4
  26.7 0.0 copy-done.5
  26.7 0.0 copy-done.6
  26.7 0.0 copy-start.2
  26.7 0.0 copy-start.3
  26.8 0.0 copy-start.7
  26.8 0.8 %products.1 = bf16[16,128,128]{2,1,0:T(8,128)(2,1)S(1)} custom-call(s32[32]{0:T(128)S(1)} %copy-done.4, s32[32]{0:T(128)S(1)} %copy-done.5, s32[32]{0:T(128)S(1)} %copy-done.6, bf16[16,96,128]{2,1,0:T(8,128)(2,1)S(1)} %all_to_all.15.held), custom_call_target="tpu_custom_call" | custom-call | tf_op jit(solution)/shard_map/products/pallas_call | solution.py:160
  27.6 0.0 copy-start
  27.6 0.0 copy-start.1
  27.6 20.2 %all_to_all.16.products = bf16[16,128,128]{2,1,0:T(8,128)(2,1)S(1)} all-to-all(bf16[16,128,128]{2,1,0:T(8,128)(2,1)S(1)} %products.1), channel_id=1, replica_groups=mesh['src'=32,'tile'=16] {'tile'}, dimensions={0} | all-to-all | bytes 1048576 | tf_op jit(solution)/shard_map/all_to_all | solution.py:168
  47.8 0.0 copy-done.2
  47.8 0.0 copy-done.3
  47.8 0.0 copy-done.7
  47.8 1.3 %images.1 = bf16[32,8,256]{2,1,0:T(8,128)(2,1)S(1)} custom-call(s32[4]{0:T(128)S(1)} %copy-done.7, bf16[16,128,128]{2,1,0:T(8,128)(2,1)S(1)} %all_to_all.16.products, bf16[256,512]{1,0:T(8,128)(2,1)S(1)} %copy-done.3, bf16[2,256,256]{2,1,0:T(8,128)(2,1)S(1)} %copy-done.2), custom_call_target="tpu_custom_call" | custom-call | tf_op jit(solution)/shard_map/images/pallas_call | solution.py:170
  49.1 21.4 %all_to_all.17.parts = bf16[32,8,256]{2,1,0:T(8,128)(2,1)S(1)} all-to-all(bf16[32,8,256]{2,1,0:T(8,128)(2,1)S(1)} %images.1), channel_id=1, replica_groups=mesh['src'=32,'tile'=16] {'src'}, dimensions={0} | all-to-all | bytes 262144 | tf_op jit(solution)/shard_map/all_to_all | solution.py:178
  70.5 0.0 copy-done
  70.5 0.0 copy-done.1
  70.5 1.1 %finish.1 = f32[4,2,2048]{2,1,0:T(2,128)} custom-call(bf16[32,8,256]{2,1,0:T(8,128)(2,1)S(1)} %all_to_all.17.parts, bf16[256,2048]{1,0:T(8,128)(2,1)S(1)} %copy-done.1, bf16[256,2048]{1,0:T(8,128)(2,1)S(1)} %copy-done), custom_call_target="tpu_custom_call" | custom-call | tf_op jit(solution)/shard_map/finish/pallas_call | solution.py:181
Async XLA Ops:
  1.8 24.9 %copy-start.4 = (s32[32]{0:T(128)S(1)}, s32[32]{0:T(128)}, u32[]{:S(2)}) copy-start(s32[32]{0:T(128)} %assignment.1) | copy-start | bytes 388
  1.8 24.9 %copy-start.5 = (s32[32]{0:T(128)S(1)}, s32[32]{0:T(128)}, u32[]{:S(2)}) copy-start(s32[32]{0:T(128)} %zone_of.1) | copy-start | bytes 388
  1.8 24.9 %copy-start.6 = (s32[32]{0:T(128)S(1)}, s32[32]{0:T(128)}, u32[]{:S(2)}) copy-start(s32[32]{0:T(128)} %density.1) | copy-start | bytes 388
  26.7 21.1 %copy-start.2 = (bf16[2,256,256]{2,1,0:T(8,128)(2,1)S(1)}, bf16[2,256,256]{2,1,0:T(8,128)(2,1)}, u32[]{:S(2)}) copy-start(bf16[2,256,256]{2,1,0:T(8,128)(2,1)} %constant.9.clone.rows) | copy-start | bytes 786436
  26.7 21.1 %copy-start.3 = (bf16[256,512]{1,0:T(8,128)(2,1)S(1)}, bf16[256,512]{1,0:T(8,128)(2,1)}, u32[]{:S(2)}) copy-start(bf16[256,512]{1,0:T(8,128)(2,1)} %constant.8.clone.columns) | copy-start | bytes 786436
  26.8 21.0 %copy-start.7 = (s32[4]{0:T(128)S(1)}, s32[4]{0:T(128)}, u32[]{:S(2)}) copy-start(s32[4]{0:T(128)} %weights.1) | copy-start | bytes 52
  27.6 42.9 %copy-start = (bf16[256,2048]{1,0:T(8,128)(2,1)S(1)}, bf16[256,2048]{1,0:T(8,128)(2,1)}, u32[]{:S(2)}) copy-start(bf16[256,2048]{1,0:T(8,128)(2,1)} %constant.11.clone.low) | copy-start | bytes 3145732
  27.6 42.9 %copy-start.1 = (bf16[256,2048]{1,0:T(8,128)(2,1)S(1)}, bf16[256,2048]{1,0:T(8,128)(2,1)}, u32[]{:S(2)}) copy-start(bf16[256,2048]{1,0:T(8,128)(2,1)} %constant.10.clone.high) | copy-start | bytes 3145732

commit v4 on v3

--- a/solution.py
+++ b/solution.py
@@ -153,8 +153,12 @@
         in_specs=[hbm, hbm],
         out_specs=blocks,
         scratch_shapes=[pltpu.SemaphoreType.DMA((12,))],
+        compiler_params=params,
         name="layout",
-    )(pupils.reshape(sources, 2, devices, 8, K), spectra.reshape(2, 2, devices, 8, K))
+    )(
+        pltpu.with_memory_space_constraint(pupils.reshape(sources, 2, devices, 8, K), pltpu.HBM),
+        pltpu.with_memory_space_constraint(spectra.reshape(2, 2, devices, 8, K), pltpu.HBM),
+    )
     held = lax.all_to_all(laid.reshape(devices, 96, K), "tile", 0, 0, tiled=True)
 
     products = pl.pallas_call(

time: 71.9 us -> 70.9 us (0.986)
  Pallas kernels: 4.96 us -> 4.22 us
    all_to_all x1, blocking collectives: 24.9 us -> 24 us  [shards(): lax.all_to_all(laid.reshape(devices, 96, K), 'tile', 0, 0, tiled=True)]
    pallas_call x1, Pallas kernels: 1.78 us -> 1.04 us  [shards(): pl.pallas_call(layout_kernel, out_shape=jax.ShapeDtypeStruct((devices, 12...]
where the time goes in v4:
time: 70.9 us; the launch traced here: 70.6 us
  blocking collectives  66.2 us (93%)
  Pallas kernels  4.22 us (6%)
    all_to_all x1, blocking collectives, shards(): lax.all_to_all(laid.reshape(devices, 96, K), 'tile', 0, 0, tiled=True)  24 us
    all_to_all x1, blocking collectives, shards(): parts = lax.all_to_all(image, 'src', 0, 0, tiled=True)  22.1 us
    all_to_all x1, blocking collectives, shards(): products = lax.all_to_all(products, 'tile', 0, 0, tiled=True)  20.2 us

profile of v4, /device:TPU:1, one launch (start us, length us, event | category | flops | bytes accessed | tf_op | source)
XLA Modules:
  0.0 70.6 jit_solution(14097985852565552891)
XLA Ops:
  0.0 1.0 %layout.1 = bf16[16,12,8,128]{3,2,1,0:T(8,128)(2,1)S(1)} custom-call(bf16[4,2,16,8,128]{4,3,2,1,0:T(8,128)(2,1)} %bitcast.4, bf16[2,2,16,8,128]{4,3,2,1,0:T(8,128)(2,1)} %bitcast.5), custom_call_target="tpu_custom_call" | custom-call | tf_op jit(solution)/shard_map/layout/pallas_call | solution.py:150
  1.0 0.0 copy-start.4
  1.1 0.0 copy-start.5
  1.1 0.0 copy-start.6
  1.1 24.0 %all_to_all.15.held = bf16[16,96,128]{2,1,0:T(8,128)(2,1)S(1)} all-to-all(bf16[16,96,128]{2,1,0:T(8,128)(2,1)S(1)} %bitcast.3), channel_id=1, replica_groups=mesh['src'=32,'tile'=16] {'tile'}, dimensions={0} | all-to-all | bytes 786432 | tf_op jit(solution)/shard_map/all_to_all | solution.py:162
  25.1 0.0 copy-done.4
  25.1 0.0 copy-done.5
  25.1 0.0 copy-done.6
  25.1 0.0 copy-start.2
  25.1 0.0 copy-start.3
  25.1 0.0 copy-start.7
  25.1 0.8 %products.1 = bf16[16,128,128]{2,1,0:T(8,128)(2,1)S(1)} custom-call(s32[32]{0:T(128)S(1)} %copy-done.4, s32[32]{0:T(128)S(1)} %copy-done.5, s32[32]{0:T(128)S(1)} %copy-done.6, bf16[16,96,128]{2,1,0:T(8,128)(2,1)S(1)} %all_to_all.15.held), custom_call_target="tpu_custom_call" | custom-call | tf_op jit(solution)/shard_map/products/pallas_call | solution.py:164
  26.0 0.0 copy-start
  26.0 0.0 copy-start.1
  26.0 20.2 %all_to_all.16.products = bf16[16,128,128]{2,1,0:T(8,128)(2,1)S(1)} all-to-all(bf16[16,128,128]{2,1,0:T(8,128)(2,1)S(1)} %products.1), channel_id=1, replica_groups=mesh['src'=32,'tile'=16] {'tile'}, dimensions={0} | all-to-all | bytes 1048576 | tf_op jit(solution)/shard_map/all_to_all | solution.py:172
  46.1 0.0 copy-done.2
  46.1 0.0 copy-done.3
  46.1 0.0 copy-done.7
  46.1 1.3 %images.1 = bf16[32,8,256]{2,1,0:T(8,128)(2,1)S(1)} custom-call(s32[4]{0:T(128)S(1)} %copy-done.7, bf16[16,128,128]{2,1,0:T(8,128)(2,1)S(1)} %all_to_all.16.products, bf16[256,512]{1,0:T(8,128)(2,1)S(1)} %copy-done.3, bf16[2,256,256]{2,1,0:T(8,128)(2,1)S(1)} %copy-done.2), custom_call_target="tpu_custom_call" | custom-call | tf_op jit(solution)/shard_map/images/pallas_call | solution.py:174
  47.4 22.1 %all_to_all.17.parts = bf16[32,8,256]{2,1,0:T(8,128)(2,1)S(1)} all-to-all(bf16[32,8,256]{2,1,0:T(8,128)(2,1)S(1)} %images.1), channel_id=1, replica_groups=mesh['src'=32,'tile'=16] {'src'}, dimensions={0} | all-to-all | bytes 262144 | tf_op jit(solution)/shard_map/all_to_all | solution.py:182
  69.5 0.0 copy-done
  69.5 0.0 copy-done.1
  69.5 1.1 %finish.1 = f32[4,2,2048]{2,1,0:T(2,128)} custom-call(bf16[32,8,256]{2,1,0:T(8,128)(2,1)S(1)} %all_to_all.17.parts, bf16[256,2048]{1,0:T(8,128)(2,1)S(1)} %copy-done.1, bf16[256,2048]{1,0:T(8,128)(2,1)S(1)} %copy-done), custom_call_target="tpu_custom_call" | custom-call | tf_op jit(solution)/shard_map/finish/pallas_call | solution.py:185
Async XLA Ops:
  1.0 24.0 %copy-start.4 = (s32[32]{0:T(128)S(1)}, s32[32]{0:T(128)}, u32[]{:S(2)}) copy-start(s32[32]{0:T(128)} %assignment.1) | copy-start | bytes 388
  1.1 24.0 %copy-start.5 = (s32[32]{0:T(128)S(1)}, s32[32]{0:T(128)}, u32[]{:S(2)}) copy-start(s32[32]{0:T(128)} %zone_of.1) | copy-start | bytes 388
  1.1 24.0 %copy-start.6 = (s32[32]{0:T(128)S(1)}, s32[32]{0:T(128)}, u32[]{:S(2)}) copy-start(s32[32]{0:T(128)} %density.1) | copy-start | bytes 388
  25.1 21.1 %copy-start.2 = (bf16[2,256,256]{2,1,0:T(8,128)(2,1)S(1)}, bf16[2,256,256]{2,1,0:T(8,128)(2,1)}, u32[]{:S(2)}) copy-start(bf16[2,256,256]{2,1,0:T(8,128)(2,1)} %constant.9.clone.rows) | copy-start | bytes 786436
  25.1 21.1 %copy-start.3 = (bf16[256,512]{1,0:T(8,128)(2,1)S(1)}, bf16[256,512]{1,0:T(8,128)(2,1)}, u32[]{:S(2)}) copy-start(bf16[256,512]{1,0:T(8,128)(2,1)} %constant.8.clone.columns) | copy-start | bytes 786436
  25.1 21.0 %copy-start.7 = (s32[4]{0:T(128)S(1)}, s32[4]{0:T(128)}, u32[]{:S(2)}) copy-start(s32[4]{0:T(128)} %weights.1) | copy-start | bytes 52
  26.0 43.6 %copy-start = (bf16[256,2048]{1,0:T(8,128)(2,1)S(1)}, bf16[256,2048]{1,0:T(8,128)(2,1)}, u32[]{:S(2)}) copy-start(bf16[256,2048]{1,0:T(8,128)(2,1)} %constant.11.clone.low) | copy-start | bytes 3145732
  26.0 43.6 %copy-start.1 = (bf16[256,2048]{1,0:T(8,128)(2,1)S(1)}, bf16[256,2048]{1,0:T(8,128)(2,1)}, u32[]{:S(2)}) copy-start(bf16[256,2048]{1,0:T(8,128)(2,1)} %constant.10.clone.high) | copy-start | bytes 3145732

commit v5 on v4

--- a/solution.py
+++ b/solution.py
@@ -56,8 +56,13 @@
     return high, low
 
 
-def layout_kernel(pupils, spectra, out, done):
-    copies = []
+def layout_kernel(pupils, spectra, assignment, zone_of, density, weights, out, tiles, zones, levels, shares, done):
+    copies = [
+        pltpu.make_async_copy(assignment, tiles, done.at[12]),
+        pltpu.make_async_copy(zone_of, zones, done.at[13]),
+        pltpu.make_async_copy(density, levels, done.at[14]),
+        pltpu.make_async_copy(weights, shares, done.at[15]),
+    ]
     for piece in range(12):
         source = pupils.at[piece // 2, piece % 2] if piece < 8 else spectra.at[(piece - 8) // 2, piece % 2]
         copies.append(pltpu.make_async_copy(source, out.at[:, piece], done.at[piece]))
@@ -147,17 +152,19 @@
     params = pltpu.CompilerParams(vmem_limit_bytes=VMEM_LIMIT)
 
     hbm = pl.BlockSpec(memory_space=pltpu.HBM)
-    laid = pl.pallas_call(
+    tables = [assignment, zone_of, density, weights]
+    laid, assignment, zone_of, density, weights = pl.pallas_call(
         layout_kernel,
-        out_shape=jax.ShapeDtypeStruct((devices, 12, 8, K), jnp.bfloat16),
-        in_specs=[hbm, hbm],
-        out_specs=blocks,
-        scratch_shapes=[pltpu.SemaphoreType.DMA((12,))],
+        out_shape=[jax.ShapeDtypeStruct((devices, 12, 8, K), jnp.bfloat16)] + [pltpu.SMEM(x.shape, x.dtype) for x in tables],
+        in_specs=[hbm] * 6,
+        out_specs=[blocks] + [scalars] * 4,
+        scratch_shapes=[pltpu.SemaphoreType.DMA((16,))],
         compiler_params=params,
         name="layout",
     )(
         pltpu.with_memory_space_constraint(pupils.reshape(sources, 2, devices, 8, K), pltpu.HBM),
         pltpu.with_memory_space_constraint(spectra.reshape(2, 2, devices, 8, K), pltpu.HBM),
+        *(pltpu.with_memory_space_constraint(x, pltpu.HBM) for x in tables),
     )
     held = lax.all_to_all(laid.reshape(devices, 96, K), "tile", 0, 0, tiled=True)
 

time: 70.9 us -> 69.6 us (0.982)
  Pallas kernels: 4.22 us -> 3.16 us
where the time goes in v5:
time: 69.6 us; the launch traced here: 69.3 us
  blocking collectives  66.1 us (95%)
  Pallas kernels  3.16 us (5%)
    all_to_all x1, blocking collectives, shards(): lax.all_to_all(laid.reshape(devices, 96, K), 'tile', 0, 0, tiled=True)  23.9 us
    all_to_all x1, blocking collectives, shards(): parts = lax.all_to_all(image, 'src', 0, 0, tiled=True)  22.1 us
    all_to_all x1, blocking collectives, shards(): products = lax.all_to_all(products, 'tile', 0, 0, tiled=True)  20.2 us

profile of v5, /device:TPU:1, one launch (start us, length us, event | category | flops | bytes accessed | tf_op | source)
XLA Modules:
  0.0 69.3 jit_solution(17448807806507366038)
XLA Ops:
  0.0 1.1 %layout.1 = (bf16[16,12,8,128]{3,2,1,0:T(8,128)(2,1)S(1)}, s32[32]{0:T(128)S(4)}, s32[32]{0:T(128)S(4)}, s32[32]{0:T(128)S(4)}, s32[4]{0:T(128)S(4)}) custom-call(bf16[4,2,16,8,128]{4,3,2,1,0:T(8,128)(2,1)} %bitcast.4, bf16[2,2,16,8,128]{4,3,2,1,0:T(8,128)(2,1)} %bitcast.5, s32[32]{0:T(128)} %assignment.1, s32[32]{0:T(128)} %zone_of.1, s32[32]{0:T(128)} %density.1, ...), custom_call_target="tpu_custom_call" | custom-call | tf_op jit(solution)/shard_map/layout/pallas_call | solution.py:156
  1.1 23.9 %all_to_all.15.held = bf16[16,96,128]{2,1,0:T(8,128)(2,1)S(1)} all-to-all(bf16[16,96,128]{2,1,0:T(8,128)(2,1)S(1)} %bitcast.3), channel_id=1, replica_groups=mesh['src'=32,'tile'=16] {'tile'}, dimensions={0} | all-to-all | bytes 786432 | tf_op jit(solution)/shard_map/all_to_all | solution.py:169
  24.9 0.0 copy-start.2
  24.9 0.0 copy-start.3
  24.9 0.3 products.1
  25.2 0.0 copy-start
  25.2 0.0 copy-start.1
  25.3 20.2 %all_to_all.16.products = bf16[16,128,128]{2,1,0:T(8,128)(2,1)S(1)} all-to-all(bf16[16,128,128]{2,1,0:T(8,128)(2,1)S(1)} %products.1), channel_id=1, replica_groups=mesh['src'=32,'tile'=16] {'tile'}, dimensions={0} | all-to-all | bytes 1048576 | tf_op jit(solution)/shard_map/all_to_all | solution.py:179
  45.4 0.0 copy-done.2
  45.4 0.0 copy-done.3
  45.4 0.7 %images.1 = bf16[32,8,256]{2,1,0:T(8,128)(2,1)S(1)} custom-call(s32[4]{0:T(128)S(4)} %get-tuple-element.10.weights, bf16[16,128,128]{2,1,0:T(8,128)(2,1)S(1)} %all_to_all.16.products, bf16[256,512]{1,0:T(8,128)(2,1)S(1)} %copy-done.3, bf16[2,256,256]{2,1,0:T(8,128)(2,1)S(1)} %copy-done.2), custom_call_target="tpu_custom_call" | custom-call | tf_op jit(solution)/shard_map/images/pallas_call | solution.py:181
  46.2 22.1 %all_to_all.17.parts = bf16[32,8,256]{2,1,0:T(8,128)(2,1)S(1)} all-to-all(bf16[32,8,256]{2,1,0:T(8,128)(2,1)S(1)} %images.1), channel_id=1, replica_groups=mesh['src'=32,'tile'=16] {'src'}, dimensions={0} | all-to-all | bytes 262144 | tf_op jit(solution)/shard_map/all_to_all | solution.py:189
  68.3 0.0 copy-done
  68.3 0.0 copy-done.1
  68.3 1.1 %finish.1 = f32[4,2,2048]{2,1,0:T(2,128)} custom-call(bf16[32,8,256]{2,1,0:T(8,128)(2,1)S(1)} %all_to_all.17.parts, bf16[256,2048]{1,0:T(8,128)(2,1)S(1)} %copy-done.1, bf16[256,2048]{1,0:T(8,128)(2,1)S(1)} %copy-done), custom_call_target="tpu_custom_call" | custom-call | tf_op jit(solution)/shard_map/finish/pallas_call | solution.py:192
Async XLA Ops:
  24.9 20.5 %copy-start.2 = (bf16[2,256,256]{2,1,0:T(8,128)(2,1)S(1)}, bf16[2,256,256]{2,1,0:T(8,128)(2,1)}, u32[]{:S(2)}) copy-start(bf16[2,256,256]{2,1,0:T(8,128)(2,1)} %constant.9.clone.rows) | copy-start | bytes 786436
  24.9 20.5 %copy-start.3 = (bf16[256,512]{1,0:T(8,128)(2,1)S(1)}, bf16[256,512]{1,0:T(8,128)(2,1)}, u32[]{:S(2)}) copy-start(bf16[256,512]{1,0:T(8,128)(2,1)} %constant.8.clone.columns) | copy-start | bytes 786436
  25.2 43.0 %copy-start = (bf16[256,2048]{1,0:T(8,128)(2,1)S(1)}, bf16[256,2048]{1,0:T(8,128)(2,1)}, u32[]{:S(2)}) copy-start(bf16[256,2048]{1,0:T(8,128)(2,1)} %constant.11.clone.low) | copy-start | bytes 3145732
  25.2 43.0 %copy-start.1 = (bf16[256,2048]{1,0:T(8,128)(2,1)S(1)}, bf16[256,2048]{1,0:T(8,128)(2,1)}, u32[]{:S(2)}) copy-start(bf16[256,2048]{1,0:T(8,128)(2,1)} %constant.10.clone.high) | copy-start | bytes 3145732

commit v6 on v5

--- a/solution.py
+++ b/solution.py
@@ -26,7 +26,9 @@
     table[0, :, 1, :SAMPLES] = np.sin(angle)
     table[1, :, 0, :SAMPLES] = -np.sin(angle)
     table[1, :, 1, :SAMPLES] = np.cos(angle)
-    return table.reshape(2 * K, 2 * WIDE).astype(ml_dtypes.bfloat16)
+    table = table.reshape(2 * K, 2 * WIDE)
+    high = table.astype(ml_dtypes.bfloat16)
+    return np.stack([high, (table - high.astype(np.float64)).astype(ml_dtypes.bfloat16)])
 
 
 def row_tables():
@@ -98,7 +100,9 @@
         real = products[:, 32 * piece : 32 * piece + 16, :].reshape(2 * K, K)
         imag = products[:, 32 * piece + 16 : 32 * piece + 32, :].reshape(2 * K, K)
         stacked.append(jnp.concatenate([real, imag], 1))
-    halves = jnp.dot(jnp.concatenate(stacked, 0), columns[...], preferred_element_type=jnp.float32)
+    stacked = jnp.concatenate(stacked, 0)
+    halves = jnp.dot(stacked, columns[0], preferred_element_type=jnp.float32)
+    halves = halves + jnp.dot(stacked, columns[1], preferred_element_type=jnp.float32)
     halves = halves.reshape(2, 2, K // 8, 2, 8, 2 * WIDE)
     images = []
     for slot in range(2):

time: 69.6 us -> 69.9 us (level)
  no operation moved by 1% of the time
where the time goes in v6:
time: 69.9 us; the launch traced here: 69.6 us
  blocking collectives  66.1 us (95%)
  Pallas kernels  3.42 us (5%)
    all_to_all x1, blocking collectives, shards(): lax.all_to_all(laid.reshape(devices, 96, K), 'tile', 0, 0, tiled=True)  23.9 us
    all_to_all x1, blocking collectives, shards(): parts = lax.all_to_all(image, 'src', 0, 0, tiled=True)  22.1 us
    all_to_all x1, blocking collectives, shards(): products = lax.all_to_all(products, 'tile', 0, 0, tiled=True)  20.2 us

profile of v6, /device:TPU:1, one launch (start us, length us, event | category | flops | bytes accessed | tf_op | source)
XLA Modules:
  0.0 69.6 jit_solution(9557178295327811628)
XLA Ops:
  0.0 1.1 %layout.1 = (bf16[16,12,8,128]{3,2,1,0:T(8,128)(2,1)S(1)}, s32[32]{0:T(128)S(4)}, s32[32]{0:T(128)S(4)}, s32[32]{0:T(128)S(4)}, s32[4]{0:T(128)S(4)}) custom-call(bf16[4,2,16,8,128]{4,3,2,1,0:T(8,128)(2,1)} %bitcast.4, bf16[2,2,16,8,128]{4,3,2,1,0:T(8,128)(2,1)} %bitcast.5, s32[32]{0:T(128)} %assignment.1, s32[32]{0:T(128)} %zone_of.1, s32[32]{0:T(128)} %density.1, ...), custom_call_target="tpu_custom_call" | custom-call | tf_op jit(solution)/shard_map/layout/pallas_call | solution.py:160
  1.1 23.9 %all_to_all.15.held = bf16[16,96,128]{2,1,0:T(8,128)(2,1)S(1)} all-to-all(bf16[16,96,128]{2,1,0:T(8,128)(2,1)S(1)} %bitcast.3), channel_id=1, replica_groups=mesh['src'=32,'tile'=16] {'tile'}, dimensions={0} | all-to-all | bytes 786432 | tf_op jit(solution)/shard_map/all_to_all | solution.py:173
  24.9 0.0 copy-start.2
  24.9 0.0 copy-start.3
  24.9 0.3 products.1
  25.2 0.0 copy-start.1
  25.2 20.2 %all_to_all.16.products = bf16[16,128,128]{2,1,0:T(8,128)(2,1)S(1)} all-to-all(bf16[16,128,128]{2,1,0:T(8,128)(2,1)S(1)} %products.1), channel_id=1, replica_groups=mesh['src'=32,'tile'=16] {'tile'}, dimensions={0} | all-to-all | bytes 1048576 | tf_op jit(solution)/shard_map/all_to_all | solution.py:183
  45.4 0.0 copy-start
  45.4 0.0 copy-done.2
  45.4 0.0 copy-done.3
  45.4 1.0 %images.1 = bf16[32,8,256]{2,1,0:T(8,128)(2,1)S(1)} custom-call(s32[4]{0:T(128)S(4)} %get-tuple-element.10.weights, bf16[16,128,128]{2,1,0:T(8,128)(2,1)S(1)} %all_to_all.16.products, bf16[2,256,512]{2,1,0:T(8,128)(2,1)S(1)} %copy-done.2, bf16[2,256,256]{2,1,0:T(8,128)(2,1)S(1)} %copy-done.3), custom_call_target="tpu_custom_call" | custom-call | tf_op jit(solution)/shard_map/images/pallas_call | solution.py:185
  46.4 22.1 %all_to_all.17.parts = bf16[32,8,256]{2,1,0:T(8,128)(2,1)S(1)} all-to-all(bf16[32,8,256]{2,1,0:T(8,128)(2,1)S(1)} %images.1), channel_id=1, replica_groups=mesh['src'=32,'tile'=16] {'src'}, dimensions={0} | all-to-all | bytes 262144 | tf_op jit(solution)/shard_map/all_to_all | solution.py:193
  68.5 0.0 copy-done.1
  68.5 0.0 copy-done
  68.5 1.1 %finish.1 = f32[4,2,2048]{2,1,0:T(2,128)} custom-call(bf16[32,8,256]{2,1,0:T(8,128)(2,1)S(1)} %all_to_all.17.parts, bf16[256,2048]{1,0:T(8,128)(2,1)S(1)} %copy-done.1, bf16[256,2048]{1,0:T(8,128)(2,1)S(1)} %copy-done), custom_call_target="tpu_custom_call" | custom-call | tf_op jit(solution)/shard_map/finish/pallas_call | solution.py:196
Async XLA Ops:
  24.9 20.5 %copy-start.2 = (bf16[2,256,512]{2,1,0:T(8,128)(2,1)S(1)}, bf16[2,256,512]{2,1,0:T(8,128)(2,1)}, u32[]{:S(2)}) copy-start(bf16[2,256,512]{2,1,0:T(8,128)(2,1)} %constant.8.clone.columns) | copy-start | bytes 1572868
  24.9 20.5 %copy-start.3 = (bf16[2,256,256]{2,1,0:T(8,128)(2,1)S(1)}, bf16[2,256,256]{2,1,0:T(8,128)(2,1)}, u32[]{:S(2)}) copy-start(bf16[2,256,256]{2,1,0:T(8,128)(2,1)} %constant.9.clone.rows) | copy-start | bytes 786436
  25.2 43.3 %copy-start.1 = (bf16[256,2048]{1,0:T(8,128)(2,1)S(1)}, bf16[256,2048]{1,0:T(8,128)(2,1)}, u32[]{:S(2)}) copy-start(bf16[256,2048]{1,0:T(8,128)(2,1)} %constant.10.clone.high) | copy-start | bytes 3145732
  45.4 23.1 %copy-start = (bf16[256,2048]{1,0:T(8,128)(2,1)S(1)}, bf16[256,2048]{1,0:T(8,128)(2,1)}, u32[]{:S(2)}) copy-start(bf16[256,2048]{1,0:T(8,128)(2,1)} %constant.11.clone.low) | copy-start | bytes 3145732

commit v7 on v5

--- a/solution.py
+++ b/solution.py
@@ -13,14 +13,15 @@
 NPIX = 2048
 ROWS = 128
 SAMPLES = 255
+OFFSET = 0.24825
 WIDE = 256
 VMEM_LIMIT = 48 * 1024 * 1024
 
 
 def sample_table():
     freq = np.arange(K) - K // 2
-    point = np.arange(SAMPLES)
-    angle = np.mod(freq[:, None] * point[None, :], SAMPLES) * (2.0 * math.pi / SAMPLES)
+    point = np.arange(SAMPLES) + OFFSET
+    angle = freq[:, None] * point[None, :] * (2.0 * math.pi / SAMPLES)
     table = np.zeros((2, K, 2, WIDE))
     table[0, :, 0, :SAMPLES] = np.cos(angle)
     table[0, :, 1, :SAMPLES] = np.sin(angle)
@@ -45,7 +46,7 @@
 
 
 def interpolation_table():
-    theta = 2.0 * math.pi * (np.arange(NPIX)[None, :] / NPIX - np.arange(SAMPLES)[:, None] / SAMPLES)
+    theta = 2.0 * math.pi * (np.arange(NPIX)[None, :] / NPIX - (np.arange(SAMPLES)[:, None] + OFFSET) / SAMPLES)
     half = np.sin(theta / 2)
     safe = np.where(np.abs(half) < 1e-12, 1.0, half)
     kernel = np.where(np.abs(half) < 1e-12, 1.0, np.sin(SAMPLES * theta / 2) / (SAMPLES * safe))

time: 69.6 us -> 69.6 us (level)
  no operation moved by 1% of the time
where the time goes in v7:
time: 69.6 us; the launch traced here: 69.3 us
  blocking collectives  66.1 us (95%)
  Pallas kernels  3.16 us (5%)
    all_to_all x1, blocking collectives, shards(): lax.all_to_all(laid.reshape(devices, 96, K), 'tile', 0, 0, tiled=True)  23.9 us
    all_to_all x1, blocking collectives, shards(): parts = lax.all_to_all(image, 'src', 0, 0, tiled=True)  22.1 us
    all_to_all x1, blocking collectives, shards(): products = lax.all_to_all(products, 'tile', 0, 0, tiled=True)  20.2 us

profile of v7, /device:TPU:1, one launch (start us, length us, event | category | flops | bytes accessed | tf_op | source)
XLA Modules:
  0.0 69.3 jit_solution(15775267440071987112)
XLA Ops:
  0.0 1.1 %layout.1 = (bf16[16,12,8,128]{3,2,1,0:T(8,128)(2,1)S(1)}, s32[32]{0:T(128)S(4)}, s32[32]{0:T(128)S(4)}, s32[32]{0:T(128)S(4)}, s32[4]{0:T(128)S(4)}) custom-call(bf16[4,2,16,8,128]{4,3,2,1,0:T(8,128)(2,1)} %bitcast.4, bf16[2,2,16,8,128]{4,3,2,1,0:T(8,128)(2,1)} %bitcast.5, s32[32]{0:T(128)} %assignment.1, s32[32]{0:T(128)} %zone_of.1, s32[32]{0:T(128)} %density.1, ...), custom_call_target="tpu_custom_call" | custom-call | tf_op jit(solution)/shard_map/layout/pallas_call | solution.py:157
  1.1 23.9 %all_to_all.15.held = bf16[16,96,128]{2,1,0:T(8,128)(2,1)S(1)} all-to-all(bf16[16,96,128]{2,1,0:T(8,128)(2,1)S(1)} %bitcast.3), channel_id=1, replica_groups=mesh['src'=32,'tile'=16] {'tile'}, dimensions={0} | all-to-all | bytes 786432 | tf_op jit(solution)/shard_map/all_to_all | solution.py:170
  24.9 0.0 copy-start.2
  24.9 0.0 copy-start.3
  24.9 0.3 products.1
  25.2 0.0 copy-start
  25.2 0.0 copy-start.1
  25.3 20.2 %all_to_all.16.products = bf16[16,128,128]{2,1,0:T(8,128)(2,1)S(1)} all-to-all(bf16[16,128,128]{2,1,0:T(8,128)(2,1)S(1)} %products.1), channel_id=1, replica_groups=mesh['src'=32,'tile'=16] {'tile'}, dimensions={0} | all-to-all | bytes 1048576 | tf_op jit(solution)/shard_map/all_to_all | solution.py:180
  45.4 0.0 copy-done.2
  45.4 0.0 copy-done.3
  45.4 0.7 %images.1 = bf16[32,8,256]{2,1,0:T(8,128)(2,1)S(1)} custom-call(s32[4]{0:T(128)S(4)} %get-tuple-element.10.weights, bf16[16,128,128]{2,1,0:T(8,128)(2,1)S(1)} %all_to_all.16.products, bf16[256,512]{1,0:T(8,128)(2,1)S(1)} %copy-done.3, bf16[2,256,256]{2,1,0:T(8,128)(2,1)S(1)} %copy-done.2), custom_call_target="tpu_custom_call" | custom-call | tf_op jit(solution)/shard_map/images/pallas_call | solution.py:182
  46.2 22.1 %all_to_all.17.parts = bf16[32,8,256]{2,1,0:T(8,128)(2,1)S(1)} all-to-all(bf16[32,8,256]{2,1,0:T(8,128)(2,1)S(1)} %images.1), channel_id=1, replica_groups=mesh['src'=32,'tile'=16] {'src'}, dimensions={0} | all-to-all | bytes 262144 | tf_op jit(solution)/shard_map/all_to_all | solution.py:190
  68.3 0.0 copy-done
  68.3 0.0 copy-done.1
  68.3 1.1 %finish.1 = f32[4,2,2048]{2,1,0:T(2,128)} custom-call(bf16[32,8,256]{2,1,0:T(8,128)(2,1)S(1)} %all_to_all.17.parts, bf16[256,2048]{1,0:T(8,128)(2,1)S(1)} %copy-done.1, bf16[256,2048]{1,0:T(8,128)(2,1)S(1)} %copy-done), custom_call_target="tpu_custom_call" | custom-call | tf_op jit(solution)/shard_map/finish/pallas_call | solution.py:193
Async XLA Ops:
  24.9 20.5 %copy-start.2 = (bf16[2,256,256]{2,1,0:T(8,128)(2,1)S(1)}, bf16[2,256,256]{2,1,0:T(8,128)(2,1)}, u32[]{:S(2)}) copy-start(bf16[2,256,256]{2,1,0:T(8,128)(2,1)} %constant.9.clone.rows) | copy-start | bytes 786436
  24.9 20.5 %copy-start.3 = (bf16[256,512]{1,0:T(8,128)(2,1)S(1)}, bf16[256,512]{1,0:T(8,128)(2,1)}, u32[]{:S(2)}) copy-start(bf16[256,512]{1,0:T(8,128)(2,1)} %constant.8.clone.columns) | copy-start | bytes 786436
  25.2 43.0 %copy-start = (bf16[256,2048]{1,0:T(8,128)(2,1)S(1)}, bf16[256,2048]{1,0:T(8,128)(2,1)}, u32[]{:S(2)}) copy-start(bf16[256,2048]{1,0:T(8,128)(2,1)} %constant.11.clone.low) | copy-start | bytes 3145732
  25.2 43.0 %copy-start.1 = (bf16[256,2048]{1,0:T(8,128)(2,1)S(1)}, bf16[256,2048]{1,0:T(8,128)(2,1)}, u32[]{:S(2)}) copy-start(bf16[256,2048]{1,0:T(8,128)(2,1)} %constant.10.clone.high) | copy-start | bytes 3145732

commit v8 on v7

--- a/solution.py
+++ b/solution.py
@@ -52,9 +52,7 @@
     kernel = np.where(np.abs(half) < 1e-12, 1.0, np.sin(SAMPLES * theta / 2) / (SAMPLES * safe))
     table = np.zeros((WIDE, NPIX))
     table[:SAMPLES] = kernel
-    high = table.astype(ml_dtypes.bfloat16)
-    low = (table - high.astype(np.float64)).astype(ml_dtypes.bfloat16)
-    return high, low
+    return table.astype(ml_dtypes.bfloat16)
 
 
 def layout_kernel(pupils, spectra, assignment, zone_of, density, weights, out, tiles, zones, levels, shares, done):
@@ -123,19 +121,21 @@
     out[...] = jnp.stack([lower, upper], 1).reshape(ROWS // 4, 8, WIDE).astype(out.dtype)
 
 
-def finish_kernel(parts, high, low, out, held, done):
+def finish_kernel(parts, table, out, held, done):
     summed = jnp.sum(parts[...].astype(jnp.float32), 0)
     total = summed[:, SAMPLES:]
-    coarse = summed.astype(jnp.bfloat16)
-    fine = (summed - coarse.astype(jnp.float32)).astype(jnp.bfloat16)
+    inside = lax.broadcasted_iota(jnp.int32, summed.shape, 1) < SAMPLES
+    mean = jnp.sum(jnp.where(inside, summed, 0.0), 1, keepdims=True) * (1.0 / SAMPLES)
+    rest = jnp.where(inside, summed - mean, 0.0)
+    coarse = rest.astype(jnp.bfloat16)
+    fine = (rest - coarse.astype(jnp.float32)).astype(jnp.bfloat16)
     both = jnp.concatenate([coarse, fine], 0)
     copies = []
-    width = NPIX // 4
-    for piece in range(4):
+    width = NPIX // 2
+    for piece in range(2):
         cut = pl.ds(width * piece, width)
-        by_high = jnp.dot(both, high[:, cut], preferred_element_type=jnp.float32)
-        by_low = jnp.dot(coarse, low[:, cut], preferred_element_type=jnp.float32)
-        result = (by_high[:8] + by_high[8:] + by_low) / total
+        spread = jnp.dot(both, table[:, cut], preferred_element_type=jnp.float32)
+        result = (mean + (spread[:8] + spread[8:])) / total
         for row in range(4):
             held[row, :, cut] = result[2 * row : 2 * row + 2]
         copy = pltpu.make_async_copy(held.at[:, :, cut], out.at[:, :, cut], done.at[piece])
@@ -189,16 +189,15 @@
     )(weights, products, jnp.asarray(sample_table()), jnp.asarray(row_tables()))
     parts = lax.all_to_all(image, "src", 0, 0, tiled=True)
 
-    high, low = interpolation_table()
     return pl.pallas_call(
         finish_kernel,
         out_shape=jax.ShapeDtypeStruct((4, 2, NPIX), jnp.float32),
-        in_specs=[blocks] * 3,
+        in_specs=[blocks] * 2,
         out_specs=hbm,
         scratch_shapes=[pltpu.VMEM((4, 2, NPIX), jnp.float32), pltpu.SemaphoreType.DMA((4,))],
         compiler_params=params,
         name="finish",
-    )(parts, jnp.asarray(high), jnp.asarray(low))
+    )(parts, jnp.asarray(interpolation_table()))
 
 
 def solution(mesh):

time: 69.6 us -> 69.5 us (level)
  no operation moved by 1% of the time
where the time goes in v8:
time: 69.5 us; the launch traced here: 69.2 us
  blocking collectives  66.1 us (95%)
  Pallas kernels  3.1 us (4%)
    all_to_all x1, blocking collectives, shards(): lax.all_to_all(laid.reshape(devices, 96, K), 'tile', 0, 0, tiled=True)  23.9 us
    all_to_all x1, blocking collectives, shards(): parts = lax.all_to_all(image, 'src', 0, 0, tiled=True)  22.1 us
    all_to_all x1, blocking collectives, shards(): products = lax.all_to_all(products, 'tile', 0, 0, tiled=True)  20.2 us

profile of v8, /device:TPU:1, one launch (start us, length us, event | category | flops | bytes accessed | tf_op | source)
XLA Modules:
  0.0 69.2 jit_solution(7682641283104917825)
XLA Ops:
  0.0 1.1 %layout.1 = (bf16[16,12,8,128]{3,2,1,0:T(8,128)(2,1)S(1)}, s32[32]{0:T(128)S(4)}, s32[32]{0:T(128)S(4)}, s32[32]{0:T(128)S(4)}, s32[4]{0:T(128)S(4)}) custom-call(bf16[4,2,16,8,128]{4,3,2,1,0:T(8,128)(2,1)} %bitcast.4, bf16[2,2,16,8,128]{4,3,2,1,0:T(8,128)(2,1)} %bitcast.5, s32[32]{0:T(128)} %assignment.1, s32[32]{0:T(128)} %zone_of.1, s32[32]{0:T(128)} %density.1, ...), custom_call_target="tpu_custom_call" | custom-call | tf_op jit(solution)/shard_map/layout/pallas_call | solution.py:157
  1.1 23.9 %all_to_all.15.held = bf16[16,96,128]{2,1,0:T(8,128)(2,1)S(1)} all-to-all(bf16[16,96,128]{2,1,0:T(8,128)(2,1)S(1)} %bitcast.3), channel_id=1, replica_groups=mesh['src'=32,'tile'=16] {'tile'}, dimensions={0} | all-to-all | bytes 786432 | tf_op jit(solution)/shard_map/all_to_all | solution.py:170
  24.9 0.0 copy-start.1
  24.9 0.0 copy-start.2
  24.9 0.3 products.1
  25.2 0.0 copy-start
  25.2 20.2 %all_to_all.16.products = bf16[16,128,128]{2,1,0:T(8,128)(2,1)S(1)} all-to-all(bf16[16,128,128]{2,1,0:T(8,128)(2,1)S(1)} %products.1), channel_id=1, replica_groups=mesh['src'=32,'tile'=16] {'tile'}, dimensions={0} | all-to-all | bytes 1048576 | tf_op jit(solution)/shard_map/all_to_all | solution.py:180
  45.4 0.0 copy-done.1
  45.4 0.0 copy-done.2
  45.4 0.7 %images.1 = bf16[32,8,256]{2,1,0:T(8,128)(2,1)S(1)} custom-call(s32[4]{0:T(128)S(4)} %get-tuple-element.10.weights, bf16[16,128,128]{2,1,0:T(8,128)(2,1)S(1)} %all_to_all.16.products, bf16[256,512]{1,0:T(8,128)(2,1)S(1)} %copy-done.2, bf16[2,256,256]{2,1,0:T(8,128)(2,1)S(1)} %copy-done.1), custom_call_target="tpu_custom_call" | custom-call | tf_op jit(solution)/shard_map/images/pallas_call | solution.py:182
  46.2 22.1 %all_to_all.17.parts = bf16[32,8,256]{2,1,0:T(8,128)(2,1)S(1)} all-to-all(bf16[32,8,256]{2,1,0:T(8,128)(2,1)S(1)} %images.1), channel_id=1, replica_groups=mesh['src'=32,'tile'=16] {'src'}, dimensions={0} | all-to-all | bytes 262144 | tf_op jit(solution)/shard_map/all_to_all | solution.py:190
  68.2 0.0 copy-done
  68.2 1.0 %finish.1 = f32[4,2,2048]{2,1,0:T(2,128)} custom-call(bf16[32,8,256]{2,1,0:T(8,128)(2,1)S(1)} %all_to_all.17.parts, bf16[256,2048]{1,0:T(8,128)(2,1)S(1)} %copy-done), custom_call_target="tpu_custom_call" | custom-call | tf_op jit(solution)/shard_map/finish/pallas_call | solution.py:192
Async XLA Ops:
  24.9 20.5 %copy-start.1 = (bf16[2,256,256]{2,1,0:T(8,128)(2,1)S(1)}, bf16[2,256,256]{2,1,0:T(8,128)(2,1)}, u32[]{:S(2)}) copy-start(bf16[2,256,256]{2,1,0:T(8,128)(2,1)} %constant.7.clone.rows) | copy-start | bytes 786436
  24.9 20.5 %copy-start.2 = (bf16[256,512]{1,0:T(8,128)(2,1)S(1)}, bf16[256,512]{1,0:T(8,128)(2,1)}, u32[]{:S(2)}) copy-start(bf16[256,512]{1,0:T(8,128)(2,1)} %constant.6.clone.columns) | copy-start | bytes 786436
  25.2 43.0 %copy-start = (bf16[256,2048]{1,0:T(8,128)(2,1)S(1)}, bf16[256,2048]{1,0:T(8,128)(2,1)}, u32[]{:S(2)}) copy-start(bf16[256,2048]{1,0:T(8,128)(2,1)} %constant.8.clone.table) | copy-start | bytes 3145732

commit v9 on v7

--- a/solution.py
+++ b/solution.py
@@ -52,9 +52,9 @@
     kernel = np.where(np.abs(half) < 1e-12, 1.0, np.sin(SAMPLES * theta / 2) / (SAMPLES * safe))
     table = np.zeros((WIDE, NPIX))
     table[:SAMPLES] = kernel
-    high = table.astype(ml_dtypes.bfloat16)
-    low = (table - high.astype(np.float64)).astype(ml_dtypes.bfloat16)
-    return high, low
+    rounded = table.astype(ml_dtypes.bfloat16)
+    missing = 1.0 - rounded.astype(np.float64).sum(0, keepdims=True)
+    return rounded, missing.astype(np.float32)
 
 
 def layout_kernel(pupils, spectra, assignment, zone_of, density, weights, out, tiles, zones, levels, shares, done):
@@ -123,19 +123,20 @@
     out[...] = jnp.stack([lower, upper], 1).reshape(ROWS // 4, 8, WIDE).astype(out.dtype)
 
 
-def finish_kernel(parts, high, low, out, held, done):
+def finish_kernel(parts, table, missing, out, held, done):
     summed = jnp.sum(parts[...].astype(jnp.float32), 0)
     total = summed[:, SAMPLES:]
     coarse = summed.astype(jnp.bfloat16)
     fine = (summed - coarse.astype(jnp.float32)).astype(jnp.bfloat16)
     both = jnp.concatenate([coarse, fine], 0)
+    inside = lax.broadcasted_iota(jnp.int32, summed.shape, 1) < SAMPLES
+    mean = jnp.sum(jnp.where(inside, summed, 0.0), 1, keepdims=True) * (1.0 / SAMPLES)
     copies = []
     width = NPIX // 4
     for piece in range(4):
         cut = pl.ds(width * piece, width)
-        by_high = jnp.dot(both, high[:, cut], preferred_element_type=jnp.float32)
-        by_low = jnp.dot(coarse, low[:, cut], preferred_element_type=jnp.float32)
-        result = (by_high[:8] + by_high[8:] + by_low) / total
+        spread = jnp.dot(both, table[:, cut], preferred_element_type=jnp.float32)
+        result = (mean * missing[:, cut] + (spread[:8] + spread[8:])) / total
         for row in range(4):
             held[row, :, cut] = result[2 * row : 2 * row + 2]
         copy = pltpu.make_async_copy(held.at[:, :, cut], out.at[:, :, cut], done.at[piece])
@@ -189,7 +190,6 @@
     )(weights, products, jnp.asarray(sample_table()), jnp.asarray(row_tables()))
     parts = lax.all_to_all(image, "src", 0, 0, tiled=True)
 
-    high, low = interpolation_table()
     return pl.pallas_call(
         finish_kernel,
         out_shape=jax.ShapeDtypeStruct((4, 2, NPIX), jnp.float32),
@@ -198,7 +198,7 @@
         scratch_shapes=[pltpu.VMEM((4, 2, NPIX), jnp.float32), pltpu.SemaphoreType.DMA((4,))],
         compiler_params=params,
         name="finish",
-    )(parts, jnp.asarray(high), jnp.asarray(low))
+    )(parts, *(jnp.asarray(x) for x in interpolation_table()))
 
 
 def solution(mesh):

time: 69.6 us -> 69.5 us (level)
  no operation moved by 1% of the time
where the time goes in v9:
time: 69.5 us; the launch traced here: 69.2 us
  blocking collectives  66.1 us (95%)
  Pallas kernels  3.04 us (4%)
    all_to_all x1, blocking collectives, shards(): lax.all_to_all(laid.reshape(devices, 96, K), 'tile', 0, 0, tiled=True)  23.9 us
    all_to_all x1, blocking collectives, shards(): parts = lax.all_to_all(image, 'src', 0, 0, tiled=True)  22.1 us
    all_to_all x1, blocking collectives, shards(): products = lax.all_to_all(products, 'tile', 0, 0, tiled=True)  20.2 us

profile of v9, /device:TPU:1, one launch (start us, length us, event | category | flops | bytes accessed | tf_op | source)
XLA Modules:
  0.0 69.2 jit_solution(10167435284739954951)
XLA Ops:
  0.0 1.1 %layout.1 = (bf16[16,12,8,128]{3,2,1,0:T(8,128)(2,1)S(1)}, s32[32]{0:T(128)S(4)}, s32[32]{0:T(128)S(4)}, s32[32]{0:T(128)S(4)}, s32[4]{0:T(128)S(4)}) custom-call(bf16[4,2,16,8,128]{4,3,2,1,0:T(8,128)(2,1)} %bitcast.4, bf16[2,2,16,8,128]{4,3,2,1,0:T(8,128)(2,1)} %bitcast.5, s32[32]{0:T(128)} %assignment.1, s32[32]{0:T(128)} %zone_of.1, s32[32]{0:T(128)} %density.1, ...), custom_call_target="tpu_custom_call" | custom-call | tf_op jit(solution)/shard_map/layout/pallas_call | solution.py:158
  1.1 23.9 %all_to_all.15.held = bf16[16,96,128]{2,1,0:T(8,128)(2,1)S(1)} all-to-all(bf16[16,96,128]{2,1,0:T(8,128)(2,1)S(1)} %bitcast.3), channel_id=1, replica_groups=mesh['src'=32,'tile'=16] {'tile'}, dimensions={0} | all-to-all | bytes 786432 | tf_op jit(solution)/shard_map/all_to_all | solution.py:171
  24.9 0.0 copy-start.1
  24.9 0.0 copy-start.2
  24.9 0.3 products.1
  25.2 0.0 copy-start
  25.2 20.2 %all_to_all.16.products = bf16[16,128,128]{2,1,0:T(8,128)(2,1)S(1)} all-to-all(bf16[16,128,128]{2,1,0:T(8,128)(2,1)S(1)} %products.1), channel_id=1, replica_groups=mesh['src'=32,'tile'=16] {'tile'}, dimensions={0} | all-to-all | bytes 1048576 | tf_op jit(solution)/shard_map/all_to_all | solution.py:181
  45.4 0.0 copy-done.1
  45.4 0.0 copy-done.2
  45.4 0.8 %images.1 = bf16[32,8,256]{2,1,0:T(8,128)(2,1)S(1)} custom-call(s32[4]{0:T(128)S(4)} %get-tuple-element.10.weights, bf16[16,128,128]{2,1,0:T(8,128)(2,1)S(1)} %all_to_all.16.products, bf16[256,512]{1,0:T(8,128)(2,1)S(1)} %copy-done.2, bf16[2,256,256]{2,1,0:T(8,128)(2,1)S(1)} %copy-done.1), custom_call_target="tpu_custom_call" | custom-call | tf_op jit(solution)/shard_map/images/pallas_call | solution.py:183
  46.2 0.0 copy-start.3
  46.2 22.1 %all_to_all.17.parts = bf16[32,8,256]{2,1,0:T(8,128)(2,1)S(1)} all-to-all(bf16[32,8,256]{2,1,0:T(8,128)(2,1)S(1)} %images.1), channel_id=1, replica_groups=mesh['src'=32,'tile'=16] {'src'}, dimensions={0} | all-to-all | bytes 262144 | tf_op jit(solution)/shard_map/all_to_all | solution.py:191
  68.3 0.0 copy-done
  68.3 0.0 copy-done.3
  68.3 0.9 %finish.1 = f32[4,2,2048]{2,1,0:T(2,128)} custom-call(bf16[32,8,256]{2,1,0:T(8,128)(2,1)S(1)} %all_to_all.17.parts, bf16[256,2048]{1,0:T(8,128)(2,1)S(1)} %copy-done, f32[1,2048]{1,0:T(1,128)S(1)} %copy-done.3), custom_call_target="tpu_custom_call" | custom-call | tf_op jit(solution)/shard_map/finish/pallas_call | solution.py:193
Async XLA Ops:
  24.9 20.5 %copy-start.1 = (bf16[2,256,256]{2,1,0:T(8,128)(2,1)S(1)}, bf16[2,256,256]{2,1,0:T(8,128)(2,1)}, u32[]{:S(2)}) copy-start(bf16[2,256,256]{2,1,0:T(8,128)(2,1)} %constant.9.clone.rows) | copy-start | bytes 786436
  24.9 20.5 %copy-start.2 = (bf16[256,512]{1,0:T(8,128)(2,1)S(1)}, bf16[256,512]{1,0:T(8,128)(2,1)}, u32[]{:S(2)}) copy-start(bf16[256,512]{1,0:T(8,128)(2,1)} %constant.8.clone.columns) | copy-start | bytes 786436
  25.2 43.0 %copy-start = (bf16[256,2048]{1,0:T(8,128)(2,1)S(1)}, bf16[256,2048]{1,0:T(8,128)(2,1)}, u32[]{:S(2)}) copy-start(bf16[256,2048]{1,0:T(8,128)(2,1)} %constant.10.clone.table) | copy-start | bytes 3145732
  46.2 22.1 %copy-start.3 = (f32[1,2048]{1,0:T(1,128)S(1)}, f32[1,2048]{1,0:T(1,128)}, u32[]{:S(2)}) copy-start(f32[1,2048]{1,0:T(1,128)} %constant.11.clone.missing) | copy-start | bytes 24580

commit v10 on v9

--- a/solution.py
+++ b/solution.py
@@ -123,7 +123,7 @@
     out[...] = jnp.stack([lower, upper], 1).reshape(ROWS // 4, 8, WIDE).astype(out.dtype)
 
 
-def finish_kernel(parts, table, missing, out, held, done):
+def finish_kernel(parts, table, missing, out):
     summed = jnp.sum(parts[...].astype(jnp.float32), 0)
     total = summed[:, SAMPLES:]
     coarse = summed.astype(jnp.bfloat16)
@@ -131,19 +131,10 @@
     both = jnp.concatenate([coarse, fine], 0)
     inside = lax.broadcasted_iota(jnp.int32, summed.shape, 1) < SAMPLES
     mean = jnp.sum(jnp.where(inside, summed, 0.0), 1, keepdims=True) * (1.0 / SAMPLES)
-    copies = []
-    width = NPIX // 4
-    for piece in range(4):
-        cut = pl.ds(width * piece, width)
-        spread = jnp.dot(both, table[:, cut], preferred_element_type=jnp.float32)
-        result = (mean * missing[:, cut] + (spread[:8] + spread[8:])) / total
-        for row in range(4):
-            held[row, :, cut] = result[2 * row : 2 * row + 2]
-        copy = pltpu.make_async_copy(held.at[:, :, cut], out.at[:, :, cut], done.at[piece])
-        copy.start()
-        copies.append(copy)
-    for copy in copies:
-        copy.wait()
+    spread = jnp.dot(both, table[...], preferred_element_type=jnp.float32)
+    result = (mean * missing[...] + (spread[:8] + spread[8:])) / total
+    for row in range(out.shape[0]):
+        out[row] = result[2 * row : 2 * row + 2]
 
 
 def shards(spectra, pupils, zone_of, density, assignment, weights):
@@ -194,8 +185,7 @@
         finish_kernel,
         out_shape=jax.ShapeDtypeStruct((4, 2, NPIX), jnp.float32),
         in_specs=[blocks] * 3,
-        out_specs=hbm,
-        scratch_shapes=[pltpu.VMEM((4, 2, NPIX), jnp.float32), pltpu.SemaphoreType.DMA((4,))],
+        out_specs=blocks,
         compiler_params=params,
         name="finish",
     )(parts, *(jnp.asarray(x) for x in interpolation_table()))

time: 69.5 us -> 69.5 us (level)
  no operation moved by 1% of the time
where the time goes in v10:
time: 69.5 us; the launch traced here: 69.2 us
  blocking collectives  66.1 us (95%)
  Pallas kernels  3.04 us (4%)
    all_to_all x1, blocking collectives, shards(): lax.all_to_all(laid.reshape(devices, 96, K), 'tile', 0, 0, tiled=True)  23.9 us
    all_to_all x1, blocking collectives, shards(): parts = lax.all_to_all(image, 'src', 0, 0, tiled=True)  22.1 us
    all_to_all x1, blocking collectives, shards(): products = lax.all_to_all(products, 'tile', 0, 0, tiled=True)  20.2 us

profile of v10, /device:TPU:1, one launch (start us, length us, event | category | flops | bytes accessed | tf_op | source)
XLA Modules:
  0.0 69.2 jit_solution(8919498081039246873)
XLA Ops:
  0.0 1.1 %layout.1 = (bf16[16,12,8,128]{3,2,1,0:T(8,128)(2,1)S(1)}, s32[32]{0:T(128)S(4)}, s32[32]{0:T(128)S(4)}, s32[32]{0:T(128)S(4)}, s32[4]{0:T(128)S(4)}) custom-call(bf16[4,2,16,8,128]{4,3,2,1,0:T(8,128)(2,1)} %bitcast.4, bf16[2,2,16,8,128]{4,3,2,1,0:T(8,128)(2,1)} %bitcast.5, s32[32]{0:T(128)} %assignment.1, s32[32]{0:T(128)} %zone_of.1, s32[32]{0:T(128)} %density.1, ...), custom_call_target="tpu_custom_call" | custom-call | tf_op jit(solution)/shard_map/layout/pallas_call | solution.py:149
  1.1 23.9 %all_to_all.15.held = bf16[16,96,128]{2,1,0:T(8,128)(2,1)S(1)} all-to-all(bf16[16,96,128]{2,1,0:T(8,128)(2,1)S(1)} %bitcast.3), channel_id=1, replica_groups=mesh['src'=32,'tile'=16] {'tile'}, dimensions={0} | all-to-all | bytes 786432 | tf_op jit(solution)/shard_map/all_to_all | solution.py:162
  24.9 0.0 copy-start.1
  24.9 0.0 copy-start.2
  24.9 0.3 products.1
  25.2 0.0 copy-start
  25.2 20.2 %all_to_all.16.products = bf16[16,128,128]{2,1,0:T(8,128)(2,1)S(1)} all-to-all(bf16[16,128,128]{2,1,0:T(8,128)(2,1)S(1)} %products.1), channel_id=1, replica_groups=mesh['src'=32,'tile'=16] {'tile'}, dimensions={0} | all-to-all | bytes 1048576 | tf_op jit(solution)/shard_map/all_to_all | solution.py:172
  45.4 0.0 copy-done.1
  45.4 0.0 copy-done.2
  45.4 0.8 %images.1 = bf16[32,8,256]{2,1,0:T(8,128)(2,1)S(1)} custom-call(s32[4]{0:T(128)S(4)} %get-tuple-element.10.weights, bf16[16,128,128]{2,1,0:T(8,128)(2,1)S(1)} %all_to_all.16.products, bf16[256,512]{1,0:T(8,128)(2,1)S(1)} %copy-done.2, bf16[2,256,256]{2,1,0:T(8,128)(2,1)S(1)} %copy-done.1), custom_call_target="tpu_custom_call" | custom-call | tf_op jit(solution)/shard_map/images/pallas_call | solution.py:174
  46.2 0.0 copy-start.3
  46.2 22.1 %all_to_all.17.parts = bf16[32,8,256]{2,1,0:T(8,128)(2,1)S(1)} all-to-all(bf16[32,8,256]{2,1,0:T(8,128)(2,1)S(1)} %images.1), channel_id=1, replica_groups=mesh['src'=32,'tile'=16] {'src'}, dimensions={0} | all-to-all | bytes 262144 | tf_op jit(solution)/shard_map/all_to_all | solution.py:182
  68.3 0.0 copy-done
  68.3 0.0 copy-done.3
  68.3 0.9 %finish.1 = f32[4,2,2048]{2,1,0:T(2,128)} custom-call(bf16[32,8,256]{2,1,0:T(8,128)(2,1)S(1)} %all_to_all.17.parts, bf16[256,2048]{1,0:T(8,128)(2,1)S(1)} %copy-done, f32[1,2048]{1,0:T(1,128)S(1)} %copy-done.3), custom_call_target="tpu_custom_call" | custom-call | tf_op jit(solution)/shard_map/finish/pallas_call | solution.py:184
Async XLA Ops:
  24.9 20.5 %copy-start.1 = (bf16[2,256,256]{2,1,0:T(8,128)(2,1)S(1)}, bf16[2,256,256]{2,1,0:T(8,128)(2,1)}, u32[]{:S(2)}) copy-start(bf16[2,256,256]{2,1,0:T(8,128)(2,1)} %constant.9.clone.rows) | copy-start | bytes 786436
  24.9 20.5 %copy-start.2 = (bf16[256,512]{1,0:T(8,128)(2,1)S(1)}, bf16[256,512]{1,0:T(8,128)(2,1)}, u32[]{:S(2)}) copy-start(bf16[256,512]{1,0:T(8,128)(2,1)} %constant.8.clone.columns) | copy-start | bytes 786436
  25.2 43.0 %copy-start = (bf16[256,2048]{1,0:T(8,128)(2,1)S(1)}, bf16[256,2048]{1,0:T(8,128)(2,1)}, u32[]{:S(2)}) copy-start(bf16[256,2048]{1,0:T(8,128)(2,1)} %constant.10.clone.table) | copy-start | bytes 3145732
  46.2 22.1 %copy-start.3 = (f32[1,2048]{1,0:T(1,128)S(1)}, f32[1,2048]{1,0:T(1,128)}, u32[]{:S(2)}) copy-start(f32[1,2048]{1,0:T(1,128)} %constant.11.clone.missing) | copy-start | bytes 24580

commit v11 on v10

--- a/solution.py
+++ b/solution.py
@@ -120,11 +120,13 @@
     second = jnp.where(last, weight_sum.astype(jnp.float32), images[1])
     lower = jnp.where(even, first, second).reshape(ROWS // 8, 8, WIDE)
     upper = jnp.where(even, pltpu.roll(first, ROWS - 1, 0), pltpu.roll(second, 1, 0)).reshape(ROWS // 8, 8, WIDE)
-    out[...] = jnp.stack([lower, upper], 1).reshape(ROWS // 4, 8, WIDE).astype(out.dtype)
+    rows_of = jnp.stack([lower, upper], 1).reshape(ROWS // 4, 8, WIDE)
+    out[...] = jnp.concatenate([rows_of[:, :, :K], rows_of[:, :, K:]], 1).astype(out.dtype)
 
 
 def finish_kernel(parts, table, missing, out):
-    summed = jnp.sum(parts[...].astype(jnp.float32), 0)
+    halves = jnp.sum(parts[...].astype(jnp.float32), 0)
+    summed = jnp.concatenate([halves[:8], halves[8:]], 1)
     total = summed[:, SAMPLES:]
     coarse = summed.astype(jnp.bfloat16)
     fine = (summed - coarse.astype(jnp.float32)).astype(jnp.bfloat16)
@@ -173,7 +175,7 @@
 
     image = pl.pallas_call(
         image_kernel,
-        out_shape=jax.ShapeDtypeStruct((ROWS // 4, 8, WIDE), jnp.bfloat16),
+        out_shape=jax.ShapeDtypeStruct((ROWS // 4, 16, K), jnp.bfloat16),
         in_specs=[scalars] + [blocks] * 3,
         out_specs=blocks,
         compiler_params=params,

time: 69.5 us -> 69.5 us (level)
  no operation moved by 1% of the time
where the time goes in v11:
time: 69.5 us; the launch traced here: 69.2 us
  blocking collectives  66.1 us (95%)
  Pallas kernels  3.04 us (4%)
    all_to_all x1, blocking collectives, shards(): lax.all_to_all(laid.reshape(devices, 96, K), 'tile', 0, 0, tiled=True)  23.9 us
    all_to_all x1, blocking collectives, shards(): parts = lax.all_to_all(image, 'src', 0, 0, tiled=True)  22.1 us
    all_to_all x1, blocking collectives, shards(): products = lax.all_to_all(products, 'tile', 0, 0, tiled=True)  20.2 us

profile of v11, /device:TPU:1, one launch (start us, length us, event | category | flops | bytes accessed | tf_op | source)
XLA Modules:
  0.0 69.2 jit_solution(1672271423907271714)
XLA Ops:
  0.0 1.1 %layout.1 = (bf16[16,12,8,128]{3,2,1,0:T(8,128)(2,1)S(1)}, s32[32]{0:T(128)S(4)}, s32[32]{0:T(128)S(4)}, s32[32]{0:T(128)S(4)}, s32[4]{0:T(128)S(4)}) custom-call(bf16[4,2,16,8,128]{4,3,2,1,0:T(8,128)(2,1)} %bitcast.4, bf16[2,2,16,8,128]{4,3,2,1,0:T(8,128)(2,1)} %bitcast.5, s32[32]{0:T(128)} %assignment.1, s32[32]{0:T(128)} %zone_of.1, s32[32]{0:T(128)} %density.1, ...), custom_call_target="tpu_custom_call" | custom-call | tf_op jit(solution)/shard_map/layout/pallas_call | solution.py:151
  1.1 23.9 %all_to_all.15.held = bf16[16,96,128]{2,1,0:T(8,128)(2,1)S(1)} all-to-all(bf16[16,96,128]{2,1,0:T(8,128)(2,1)S(1)} %bitcast.3), channel_id=1, replica_groups=mesh['src'=32,'tile'=16] {'tile'}, dimensions={0} | all-to-all | bytes 786432 | tf_op jit(solution)/shard_map/all_to_all | solution.py:164
  24.9 0.0 copy-start.1
  24.9 0.0 copy-start.2
  24.9 0.3 products.1
  25.2 0.0 copy-start
  25.2 20.2 %all_to_all.16.products = bf16[16,128,128]{2,1,0:T(8,128)(2,1)S(1)} all-to-all(bf16[16,128,128]{2,1,0:T(8,128)(2,1)S(1)} %products.1), channel_id=1, replica_groups=mesh['src'=32,'tile'=16] {'tile'}, dimensions={0} | all-to-all | bytes 1048576 | tf_op jit(solution)/shard_map/all_to_all | solution.py:174
  45.4 0.0 copy-done.1
  45.4 0.0 copy-done.2
  45.4 0.8 %images.1 = bf16[32,16,128]{2,1,0:T(8,128)(2,1)S(1)} custom-call(s32[4]{0:T(128)S(4)} %get-tuple-element.10.weights, bf16[16,128,128]{2,1,0:T(8,128)(2,1)S(1)} %all_to_all.16.products, bf16[256,512]{1,0:T(8,128)(2,1)S(1)} %copy-done.2, bf16[2,256,256]{2,1,0:T(8,128)(2,1)S(1)} %copy-done.1), custom_call_target="tpu_custom_call" | custom-call | tf_op jit(solution)/shard_map/images/pallas_call | solution.py:176
  46.2 0.0 copy-start.3
  46.2 22.1 %all_to_all.17.parts = bf16[32,16,128]{2,1,0:T(8,128)(2,1)S(1)} all-to-all(bf16[32,16,128]{2,1,0:T(8,128)(2,1)S(1)} %images.1), channel_id=1, replica_groups=mesh['src'=32,'tile'=16] {'src'}, dimensions={0} | all-to-all | bytes 262144 | tf_op jit(solution)/shard_map/all_to_all | solution.py:184
  68.3 0.0 copy-done
  68.3 0.0 copy-done.3
  68.3 0.9 %finish.1 = f32[4,2,2048]{2,1,0:T(2,128)} custom-call(bf16[32,16,128]{2,1,0:T(8,128)(2,1)S(1)} %all_to_all.17.parts, bf16[256,2048]{1,0:T(8,128)(2,1)S(1)} %copy-done, f32[1,2048]{1,0:T(1,128)S(1)} %copy-done.3), custom_call_target="tpu_custom_call" | custom-call | tf_op jit(solution)/shard_map/finish/pallas_call | solution.py:186
Async XLA Ops:
  24.9 20.5 %copy-start.1 = (bf16[2,256,256]{2,1,0:T(8,128)(2,1)S(1)}, bf16[2,256,256]{2,1,0:T(8,128)(2,1)}, u32[]{:S(2)}) copy-start(bf16[2,256,256]{2,1,0:T(8,128)(2,1)} %constant.9.clone.rows) | copy-start | bytes 786436
  24.9 20.5 %copy-start.2 = (bf16[256,512]{1,0:T(8,128)(2,1)S(1)}, bf16[256,512]{1,0:T(8,128)(2,1)}, u32[]{:S(2)}) copy-start(bf16[256,512]{1,0:T(8,128)(2,1)} %constant.8.clone.columns) | copy-start | bytes 786436
  25.2 43.0 %copy-start = (bf16[256,2048]{1,0:T(8,128)(2,1)S(1)}, bf16[256,2048]{1,0:T(8,128)(2,1)}, u32[]{:S(2)}) copy-start(bf16[256,2048]{1,0:T(8,128)(2,1)} %constant.10.clone.table) | copy-start | bytes 3145732
  46.2 22.1 %copy-start.3 = (f32[1,2048]{1,0:T(1,128)S(1)}, f32[1,2048]{1,0:T(1,128)}, u32[]{:S(2)}) copy-start(f32[1,2048]{1,0:T(1,128)} %constant.11.clone.missing) | copy-start | bytes 24580

commit v12 on v9

--- a/solution.py
+++ b/solution.py
@@ -132,8 +132,8 @@
     inside = lax.broadcasted_iota(jnp.int32, summed.shape, 1) < SAMPLES
     mean = jnp.sum(jnp.where(inside, summed, 0.0), 1, keepdims=True) * (1.0 / SAMPLES)
     copies = []
-    width = NPIX // 4
-    for piece in range(4):
+    width = NPIX // 2
+    for piece in range(2):
         cut = pl.ds(width * piece, width)
         spread = jnp.dot(both, table[:, cut], preferred_element_type=jnp.float32)
         result = (mean * missing[:, cut] + (spread[:8] + spread[8:])) / total

time: 69.5 us -> 69.5 us (level)
  no operation moved by 1% of the time
where the time goes in v12:
time: 69.5 us; the launch traced here: 69.2 us
  blocking collectives  66.1 us (95%)
  Pallas kernels  3.05 us (4%)
    all_to_all x1, blocking collectives, shards(): lax.all_to_all(laid.reshape(devices, 96, K), 'tile', 0, 0, tiled=True)  23.9 us
    all_to_all x1, blocking collectives, shards(): parts = lax.all_to_all(image, 'src', 0, 0, tiled=True)  22.1 us
    all_to_all x1, blocking collectives, shards(): products = lax.all_to_all(products, 'tile', 0, 0, tiled=True)  20.2 us

profile of v12, /device:TPU:1, one launch (start us, length us, event | category | flops | bytes accessed | tf_op | source)
XLA Modules:
  0.0 69.2 jit_solution(12194044700225500485)
XLA Ops:
  0.0 1.1 %layout.1 = (bf16[16,12,8,128]{3,2,1,0:T(8,128)(2,1)S(1)}, s32[32]{0:T(128)S(4)}, s32[32]{0:T(128)S(4)}, s32[32]{0:T(128)S(4)}, s32[4]{0:T(128)S(4)}) custom-call(bf16[4,2,16,8,128]{4,3,2,1,0:T(8,128)(2,1)} %bitcast.4, bf16[2,2,16,8,128]{4,3,2,1,0:T(8,128)(2,1)} %bitcast.5, s32[32]{0:T(128)} %assignment.1, s32[32]{0:T(128)} %zone_of.1, s32[32]{0:T(128)} %density.1, ...), custom_call_target="tpu_custom_call" | custom-call | tf_op jit(solution)/shard_map/layout/pallas_call | solution.py:158
  1.1 23.9 %all_to_all.15.held = bf16[16,96,128]{2,1,0:T(8,128)(2,1)S(1)} all-to-all(bf16[16,96,128]{2,1,0:T(8,128)(2,1)S(1)} %bitcast.3), channel_id=1, replica_groups=mesh['src'=32,'tile'=16] {'tile'}, dimensions={0} | all-to-all | bytes 786432 | tf_op jit(solution)/shard_map/all_to_all | solution.py:171
  24.9 0.0 copy-start.1
  24.9 0.0 copy-start.2
  24.9 0.3 products.1
  25.2 0.0 copy-start
  25.2 20.2 %all_to_all.16.products = bf16[16,128,128]{2,1,0:T(8,128)(2,1)S(1)} all-to-all(bf16[16,128,128]{2,1,0:T(8,128)(2,1)S(1)} %products.1), channel_id=1, replica_groups=mesh['src'=32,'tile'=16] {'tile'}, dimensions={0} | all-to-all | bytes 1048576 | tf_op jit(solution)/shard_map/all_to_all | solution.py:181
  45.4 0.0 copy-done.1
  45.4 0.0 copy-done.2
  45.4 0.8 %images.1 = bf16[32,8,256]{2,1,0:T(8,128)(2,1)S(1)} custom-call(s32[4]{0:T(128)S(4)} %get-tuple-element.10.weights, bf16[16,128,128]{2,1,0:T(8,128)(2,1)S(1)} %all_to_all.16.products, bf16[256,512]{1,0:T(8,128)(2,1)S(1)} %copy-done.2, bf16[2,256,256]{2,1,0:T(8,128)(2,1)S(1)} %copy-done.1), custom_call_target="tpu_custom_call" | custom-call | tf_op jit(solution)/shard_map/images/pallas_call | solution.py:183
  46.2 0.0 copy-start.3
  46.2 22.1 %all_to_all.17.parts = bf16[32,8,256]{2,1,0:T(8,128)(2,1)S(1)} all-to-all(bf16[32,8,256]{2,1,0:T(8,128)(2,1)S(1)} %images.1), channel_id=1, replica_groups=mesh['src'=32,'tile'=16] {'src'}, dimensions={0} | all-to-all | bytes 262144 | tf_op jit(solution)/shard_map/all_to_all | solution.py:191
  68.3 0.0 copy-done
  68.3 0.0 copy-done.3
  68.3 0.9 %finish.1 = f32[4,2,2048]{2,1,0:T(2,128)} custom-call(bf16[32,8,256]{2,1,0:T(8,128)(2,1)S(1)} %all_to_all.17.parts, bf16[256,2048]{1,0:T(8,128)(2,1)S(1)} %copy-done, f32[1,2048]{1,0:T(1,128)S(1)} %copy-done.3), custom_call_target="tpu_custom_call" | custom-call | tf_op jit(solution)/shard_map/finish/pallas_call | solution.py:193
Async XLA Ops:
  24.9 20.5 %copy-start.1 = (bf16[2,256,256]{2,1,0:T(8,128)(2,1)S(1)}, bf16[2,256,256]{2,1,0:T(8,128)(2,1)}, u32[]{:S(2)}) copy-start(bf16[2,256,256]{2,1,0:T(8,128)(2,1)} %constant.9.clone.rows) | copy-start | bytes 786436
  24.9 20.5 %copy-start.2 = (bf16[256,512]{1,0:T(8,128)(2,1)S(1)}, bf16[256,512]{1,0:T(8,128)(2,1)}, u32[]{:S(2)}) copy-start(bf16[256,512]{1,0:T(8,128)(2,1)} %constant.8.clone.columns) | copy-start | bytes 786436
  25.2 43.0 %copy-start = (bf16[256,2048]{1,0:T(8,128)(2,1)S(1)}, bf16[256,2048]{1,0:T(8,128)(2,1)}, u32[]{:S(2)}) copy-start(bf16[256,2048]{1,0:T(8,128)(2,1)} %constant.10.clone.table) | copy-start | bytes 3145732
  46.2 22.1 %copy-start.3 = (f32[1,2048]{1,0:T(1,128)S(1)}, f32[1,2048]{1,0:T(1,128)}, u32[]{:S(2)}) copy-start(f32[1,2048]{1,0:T(1,128)} %constant.11.clone.missing) | copy-start | bytes 24580

commit v13 on v10

--- a/solution.py
+++ b/solution.py
@@ -52,9 +52,7 @@
     kernel = np.where(np.abs(half) < 1e-12, 1.0, np.sin(SAMPLES * theta / 2) / (SAMPLES * safe))
     table = np.zeros((WIDE, NPIX))
     table[:SAMPLES] = kernel
-    rounded = table.astype(ml_dtypes.bfloat16)
-    missing = 1.0 - rounded.astype(np.float64).sum(0, keepdims=True)
-    return rounded, missing.astype(np.float32)
+    return table.astype(ml_dtypes.bfloat16)
 
 
 def layout_kernel(pupils, spectra, assignment, zone_of, density, weights, out, tiles, zones, levels, shares, done):
@@ -123,16 +121,17 @@
     out[...] = jnp.stack([lower, upper], 1).reshape(ROWS // 4, 8, WIDE).astype(out.dtype)
 
 
-def finish_kernel(parts, table, missing, out):
+def finish_kernel(parts, table, out):
     summed = jnp.sum(parts[...].astype(jnp.float32), 0)
     total = summed[:, SAMPLES:]
-    coarse = summed.astype(jnp.bfloat16)
-    fine = (summed - coarse.astype(jnp.float32)).astype(jnp.bfloat16)
-    both = jnp.concatenate([coarse, fine], 0)
     inside = lax.broadcasted_iota(jnp.int32, summed.shape, 1) < SAMPLES
     mean = jnp.sum(jnp.where(inside, summed, 0.0), 1, keepdims=True) * (1.0 / SAMPLES)
+    rest = jnp.where(inside, summed - mean, 0.0)
+    coarse = rest.astype(jnp.bfloat16)
+    fine = (rest - coarse.astype(jnp.float32)).astype(jnp.bfloat16)
+    both = jnp.concatenate([coarse, fine], 0)
     spread = jnp.dot(both, table[...], preferred_element_type=jnp.float32)
-    result = (mean * missing[...] + (spread[:8] + spread[8:])) / total
+    result = (mean + (spread[:8] + spread[8:])) / total
     for row in range(out.shape[0]):
         out[row] = result[2 * row : 2 * row + 2]
 
@@ -184,11 +183,11 @@
     return pl.pallas_call(
         finish_kernel,
         out_shape=jax.ShapeDtypeStruct((4, 2, NPIX), jnp.float32),
-        in_specs=[blocks] * 3,
+        in_specs=[blocks] * 2,
         out_specs=blocks,
         compiler_params=params,
         name="finish",
-    )(parts, *(jnp.asarray(x) for x in interpolation_table()))
+    )(parts, jnp.asarray(interpolation_table()))
 
 
 def solution(mesh):

time: 69.5 us -> 69.5 us (level)
  no operation moved by 1% of the time
where the time goes in v13:
time: 69.5 us; the launch traced here: 69.2 us
  blocking collectives  66.1 us (95%)
  Pallas kernels  3.08 us (4%)
    all_to_all x1, blocking collectives, shards(): lax.all_to_all(laid.reshape(devices, 96, K), 'tile', 0, 0, tiled=True)  23.9 us
    all_to_all x1, blocking collectives, shards(): parts = lax.all_to_all(image, 'src', 0, 0, tiled=True)  22.1 us
    all_to_all x1, blocking collectives, shards(): products = lax.all_to_all(products, 'tile', 0, 0, tiled=True)  20.2 us

profile of v13, /device:TPU:1, one launch (start us, length us, event | category | flops | bytes accessed | tf_op | source)
XLA Modules:
  0.0 69.2 jit_solution(6572535038385688046)
XLA Ops:
  0.0 1.1 %layout.1 = (bf16[16,12,8,128]{3,2,1,0:T(8,128)(2,1)S(1)}, s32[32]{0:T(128)S(4)}, s32[32]{0:T(128)S(4)}, s32[32]{0:T(128)S(4)}, s32[4]{0:T(128)S(4)}) custom-call(bf16[4,2,16,8,128]{4,3,2,1,0:T(8,128)(2,1)} %bitcast.4, bf16[2,2,16,8,128]{4,3,2,1,0:T(8,128)(2,1)} %bitcast.5, s32[32]{0:T(128)} %assignment.1, s32[32]{0:T(128)} %zone_of.1, s32[32]{0:T(128)} %density.1, ...), custom_call_target="tpu_custom_call" | custom-call | tf_op jit(solution)/shard_map/layout/pallas_call | solution.py:148
  1.1 23.9 %all_to_all.15.held = bf16[16,96,128]{2,1,0:T(8,128)(2,1)S(1)} all-to-all(bf16[16,96,128]{2,1,0:T(8,128)(2,1)S(1)} %bitcast.3), channel_id=1, replica_groups=mesh['src'=32,'tile'=16] {'tile'}, dimensions={0} | all-to-all | bytes 786432 | tf_op jit(solution)/shard_map/all_to_all | solution.py:161
  24.9 0.0 copy-start.1
  24.9 0.0 copy-start.2
  24.9 0.3 products.1
  25.2 0.0 copy-start
  25.2 20.2 %all_to_all.16.products = bf16[16,128,128]{2,1,0:T(8,128)(2,1)S(1)} all-to-all(bf16[16,128,128]{2,1,0:T(8,128)(2,1)S(1)} %products.1), channel_id=1, replica_groups=mesh['src'=32,'tile'=16] {'tile'}, dimensions={0} | all-to-all | bytes 1048576 | tf_op jit(solution)/shard_map/all_to_all | solution.py:171
  45.4 0.0 copy-done.1
  45.4 0.0 copy-done.2
  45.4 0.7 %images.1 = bf16[32,8,256]{2,1,0:T(8,128)(2,1)S(1)} custom-call(s32[4]{0:T(128)S(4)} %get-tuple-element.10.weights, bf16[16,128,128]{2,1,0:T(8,128)(2,1)S(1)} %all_to_all.16.products, bf16[256,512]{1,0:T(8,128)(2,1)S(1)} %copy-done.2, bf16[2,256,256]{2,1,0:T(8,128)(2,1)S(1)} %copy-done.1), custom_call_target="tpu_custom_call" | custom-call | tf_op jit(solution)/shard_map/images/pallas_call | solution.py:173
  46.2 22.1 %all_to_all.17.parts = bf16[32,8,256]{2,1,0:T(8,128)(2,1)S(1)} all-to-all(bf16[32,8,256]{2,1,0:T(8,128)(2,1)S(1)} %images.1), channel_id=1, replica_groups=mesh['src'=32,'tile'=16] {'src'}, dimensions={0} | all-to-all | bytes 262144 | tf_op jit(solution)/shard_map/all_to_all | solution.py:181
  68.2 0.0 copy-done
  68.2 1.0 %finish.1 = f32[4,2,2048]{2,1,0:T(2,128)} custom-call(bf16[32,8,256]{2,1,0:T(8,128)(2,1)S(1)} %all_to_all.17.parts, bf16[256,2048]{1,0:T(8,128)(2,1)S(1)} %copy-done), custom_call_target="tpu_custom_call" | custom-call | tf_op jit(solution)/shard_map/finish/pallas_call | solution.py:183
Async XLA Ops:
  24.9 20.5 %copy-start.1 = (bf16[2,256,256]{2,1,0:T(8,128)(2,1)S(1)}, bf16[2,256,256]{2,1,0:T(8,128)(2,1)}, u32[]{:S(2)}) copy-start(bf16[2,256,256]{2,1,0:T(8,128)(2,1)} %constant.7.clone.rows) | copy-start | bytes 786436
  24.9 20.5 %copy-start.2 = (bf16[256,512]{1,0:T(8,128)(2,1)S(1)}, bf16[256,512]{1,0:T(8,128)(2,1)}, u32[]{:S(2)}) copy-start(bf16[256,512]{1,0:T(8,128)(2,1)} %constant.6.clone.columns) | copy-start | bytes 786436
  25.2 43.0 %copy-start = (bf16[256,2048]{1,0:T(8,128)(2,1)S(1)}, bf16[256,2048]{1,0:T(8,128)(2,1)}, u32[]{:S(2)}) copy-start(bf16[256,2048]{1,0:T(8,128)(2,1)} %constant.8.clone.table) | copy-start | bytes 3145732
